TPU v7x, 512 devices: a whole 4x8x8 slice. The times are simulated.
512 devices in a mesh: prow: 4 (over x_lo, core), pcol: 128 (over z, y, x_hi).
Axes of the slice: x: 4 (x_hi: 2, x_lo: 2; x = x_hi * 2 + x_lo), y: 8, z: 8, core: 2. Of those that a mesh axis runs over, the one named last changes fastest.
Arguments:
- matrix: bfloat16 [12288, 12288], P('prow', 'pcol'), may hold values from -8 to 8
- vectors_one: bfloat16 [12288, 256], P('prow'), may hold values from -1 to 1, as said below
- factor_one: float32 [256, 256], replicated, may hold values from -1 to 2, as said below
- vectors_two: bfloat16 [12288, 256], P('prow'), may hold values from -1 to 1, as said below
- factor_two: float32 [256, 256], replicated, may hold values from -1 to 2, as said below
Outputs:
- reduced: bfloat16 [12288, 12288], P('prow', 'pcol')
Inputs may be any that keep to these rules, and one draw needn't show every extreme that they name: `vectors_one`: column j is zero in rows above 256 + j, one in row 256 + j. `vectors_two`: column j is zero in rows above 512 + j, one in row 512 + j. `factor_one`: upper triangular. `factor_two`: upper triangular.
All inputs are finite; a program needn't handle non-finite values.
Results may differ from a plain program's by a relative error of at most 0.0055.
Values may be sent and summed in bfloat16 or wider, within the bound.
A program may use at most 64 MiB of HBM per device.

v0:
```python
import jax
import jax.numpy as jnp
from jax import lax
from jax.sharding import PartitionSpec as P


def from_root(x, axis, root):
    mine = lax.axis_index(axis) == root
    return lax.psum(jnp.where(mine, x, jnp.zeros_like(x)), axis)


def body(matrix, vectors_one, factor_one, vectors_two, factor_two):
    high = lax.Precision.HIGHEST
    row_count = matrix.shape[0]
    col_count = matrix.shape[1]
    panel = factor_one.shape[0]
    row_devices = lax.axis_size("prow")
    group_size = lax.axis_size("pcol") // row_devices
    piece_rows = col_count // row_devices
    col_index = lax.axis_index("pcol")
    row_index = lax.axis_index("prow")
    offset = col_index % group_size * col_count
    owner_row = col_index // group_size

    def column_slice(values):
        return lax.dynamic_slice_in_dim(values, offset, col_count, 0)

    col_one, col_two = (
        from_root(column_slice(vectors_one), "prow", owner_row),
        from_root(column_slice(vectors_two), "prow", owner_row),
    )
    current = matrix
    for vectors, factor, col_vectors in (
        (vectors_one, factor_one, col_one),
        (vectors_two, factor_two, col_two),
    ):
        term = lax.dot_general(
            current, vectors, (((0,), (0,)), ((), ())), preferred_element_type=jnp.float32
        )
        sums = lax.psum_scatter(term, "prow", scatter_dimension=0, tiled=True)
        local_rows = lax.dynamic_slice_in_dim(
            col_vectors, row_index * piece_rows, piece_rows, 0
        ).astype(jnp.float32)
        product = jnp.dot(sums, factor, precision=high)
        inner = lax.psum(jnp.dot(local_rows.T, product, precision=high), ("prow", "pcol"))
        mine = product - 0.5 * jnp.dot(
            local_rows, jnp.dot(factor.T, inner, precision=high), precision=high
        )
        quarter = mine.astype(jnp.bfloat16)
        col_wide = lax.all_gather(quarter, "prow", axis=0, tiled=True)
        gathered = lax.all_gather(quarter, "pcol", axis=0, tiled=True)
        sectioned = gathered.reshape(row_devices, group_size, 1, piece_rows, panel)
        moved = lax.all_to_all(sectioned, "prow", split_axis=0, concat_axis=2, tiled=True)
        row_wide = moved.reshape(row_count, panel)
        update = jnp.dot(vectors, col_wide.T, preferred_element_type=jnp.float32) + jnp.dot(
            row_wide, col_vectors.T, preferred_element_type=jnp.float32
        )
        current = (current.astype(jnp.float32) - update).astype(jnp.bfloat16)
    return current


def solution(mesh):
    placed = (P("prow", "pcol"), P("prow", None), P(), P("prow", None), P())
    return jax.shard_map(
        body, mesh=mesh, in_specs=placed, out_specs=P("prow", "pcol"), check_vma=False
    )
```

profile of v0, /device:TPU:1, one launch (start us, length us, event | category | flops | bytes accessed | tf_op | source)
XLA Modules:
  0.0 962.6 jit_solution(11143385134967398014)
XLA Ops:
  6.5 2.7 fusion.18
  9.3 0.0 reduce-scatter.3.cloned.1.call-update
  9.3 0.0 all-reduce.9.cloned.1.call-start
  9.4 0.6 dynamic-slice_select_fusion.1
  10.0 1.4 dynamic-slice_select_fusion
  11.5 0.0 all-reduce.9.cloned.1.call-update
  11.5 0.0 all-reduce.5.cloned.1.call-start
  11.5 26.7 %reduce-scatter.3.cloned.1.call-done = f32[24,256]{1,0:T(8,128)} async-done(((f32[96,256]{1,0:T(8,128)}), f32[24,256]{1,0:T(8,128)}) %reduce-scatter.3.cloned.1.call-update) | async-done | bytes 24592 | tf_op jit(solution)/shard_map/reduce_scatter | solution.py:40
  38.3 1.0 fusion.19
  39.2 49.5 %all-reduce.9.cloned.1.call-done = (bf16[96,256]{1,0:T(8,128)(2,1)}, bf16[96,256]{1,0:T(8,128)(2,1)}) async-done(((bf16[96,256]{1,0:T(8,128)(2,1)}, bf16[96,256]{1,0:T(8,128)(2,1)}), (bf16[96,256]{1,0:T(8,128)(2,1)}, bf16[96,256]{1,0:T(8,128)(2,1)})) %all-reduce.9.cloned.1.call-update) | async-done | bytes 98320 | tf_op jit(solution)/shard_map/psum | solution.py:9
  88.7 1.7 fusion.12
  90.4 0.0 all-reduce.5.cloned.1.call-update
  90.5 0.0 all-gather.3.cloned.1.call-start
  90.5 271.2 %all-reduce.5.cloned.1.call-done = f32[256,256]{1,0:T(8,128)} async-done(((f32[256,256]{1,0:T(8,128)}), f32[256,256]{1,0:T(8,128)}) %all-reduce.5.cloned.1.call-update) | async-done | bytes 262160 | tf_op jit(solution)/shard_map/psum | solution.py:45
  361.7 1.5 fusion.20
  363.2 1.6 fusion.6
  364.8 0.0 all-gather.3.cloned.1.call-update
  364.8 114.2 %all-gather.3.cloned.1.call-done = bf16[3072,256]{1,0:T(8,128)(2,1)} async-done(((bf16[24,256]{1,0:T(8,128)(2,1)}), bf16[3072,256]{1,0:T(8,128)(2,1)}) %all-gather.3.cloned.1.call-update) | async-done | bytes 1572880 | tf_op jit(solution)/shard_map/all_gather | solution.py:51
  479.1 7.9 all-to-all-start
  487.0 21.0 %all_gather.12 = bf16[96,256]{1,0:T(8,128)(2,1)S(1)} all-gather(bf16[24,256]{1,0:T(8,128)(2,1)S(1)} %copy-done.11), channel_id=1, replica_groups=mesh['prow'=4,'pcol'=128] {'prow'}, dimensions={0}, use_global_device_ids=true | all-gather | bytes 61440 | tf_op jit(solution)/shard_map/all_gather | solution.py:50
  508.0 1.6 convolution_bitcast_fusion.1
  509.6 0.2 copy.9
  509.8 0.6 copy-done.10
  510.4 0.5 copy-done.6
  510.9 0.1 copy-done.7
  511.1 0.6 fusion.3
  511.7 0.0 copy-start.3
  511.7 0.8 copy-done.3
  512.5 1.0 fusion.21
  513.5 0.0 reduce-scatter.5.cloned.1.call-update
  513.6 0.0 all-reduce.7.cloned.1.call-start
  513.6 18.4 %reduce-scatter.5.cloned.1.call-done = f32[24,256]{1,0:T(8,128)} async-done(((f32[96,256]{1,0:T(8,128)}), f32[24,256]{1,0:T(8,128)}) %reduce-scatter.5.cloned.1.call-update) | async-done | bytes 24592 | tf_op jit(solution)/shard_map/reduce_scatter | solution.py:40
  532.0 1.0 fusion.22
  533.0 1.0 fusion.9
  534.0 0.0 all-reduce.7.cloned.1.call-update
  534.0 0.0 all-gather.5.cloned.1.call-start
  534.1 270.6 %all-reduce.7.cloned.1.call-done = f32[256,256]{1,0:T(8,128)} async-done(((f32[256,256]{1,0:T(8,128)}), f32[256,256]{1,0:T(8,128)}) %all-reduce.7.cloned.1.call-update) | async-done | bytes 262160 | tf_op jit(solution)/shard_map/psum | solution.py:45
  804.7 1.5 fusion.23
  806.3 0.9 fusion.7
  807.1 0.0 all-gather.5.cloned.1.call-update
  807.2 115.1 %all-gather.5.cloned.1.call-done = bf16[3072,256]{1,0:T(8,128)(2,1)} async-done(((bf16[24,256]{1,0:T(8,128)(2,1)}), bf16[3072,256]{1,0:T(8,128)(2,1)}) %all-gather.5.cloned.1.call-update) | async-done | bytes 1572880 | tf_op jit(solution)/shard_map/all_gather | solution.py:51
  922.3 7.9 all-to-all-start.1
  930.2 21.0 %all_gather.14 = bf16[96,256]{1,0:T(8,128)(2,1)S(1)} all-gather(bf16[24,256]{1,0:T(8,128)(2,1)S(1)} %copy-done.12), channel_id=1, replica_groups=mesh['prow'=4,'pcol'=128] {'prow'}, dimensions={0}, use_global_device_ids=true | all-gather | bytes 61440 | tf_op jit(solution)/shard_map/all_gather | solution.py:50
  951.2 1.6 convolution_bitcast_fusion
  952.8 0.2 copy.11
  953.0 0.9 copy-done.4
  953.9 0.4 copy-done.5
  954.3 1.4 fusion.2
  (23 shorter events, 0.0 us)
Async XLA Ops:
  6.5 31.7 %copy-start = (f32[256,256]{1,0:T(8,128)S(1)}, f32[256,256]{1,0:T(8,128)}, u32[]{:S(2)}) copy-start(f32[256,256]{1,0:T(8,128)} %param.7) | copy-start | bytes 786436
  6.5 2.9 copy-start.1
  6.5 31.7 %reduce-scatter.3.cloned.1.call-start = ((), (), s32[]{:S(2)}) async-start(), calls=%async_computation.4 | async-start | bytes 122880 | tf_op jit(solution)/shard_map/reduce_scatter | solution.py:40
  9.3 79.4 %all-reduce.9.cloned.1.call-start = ((), (), s32[]{:S(2)}) async-start(), calls=%async_computation.10 | async-start | bytes 196608 | tf_op jit(solution)/shard_map/psum | solution.py:9
  11.5 350.2 %all-reduce.5.cloned.1.call-start = ((), (), s32[]{:S(2)}) async-start(), calls=%async_computation.5 | async-start | bytes 524288 | tf_op jit(solution)/shard_map/psum | solution.py:45
  90.5 388.6 %all-gather.3.cloned.1.call-start = ((), (), s32[]{:S(2)}) async-start(), calls=%async_computation.6 | async-start | bytes 1585152 | tf_op jit(solution)/shard_map/all_gather | solution.py:51
  479.1 7.9 copy-start.11
  479.1 30.6 %all-to-all-start = ((bf16[4,32,1,24,256]{4,3,1,2,0:T(8,128)(2,1)}), bf16[4,32,1,24,256]{4,3,1,2,0:T(8,128)(2,1)S(1)}, u32[]{:S(2)}, u32[]{:S(2)}) async-start(bf16[4,32,1,24,256]{4,3,1,2,0:T(8,128)(2,1)} %bitcast.46), calls=%async_computation.1 | async-start | bytes 3145728 | tf_op jit(solution)/shard_map/all_to_all | solution.py:53
  487.0 45.0 %reduce-scatter.5.cloned.1.call-start = ((), (), s32[]{:S(2)}) async-start(), calls=%async_computation.7 | async-start | bytes 122880 | tf_op jit(solution)/shard_map/reduce_scatter | solution.py:40
  509.6 0.8 copy-start.10
  509.6 1.3 copy-start.6
  509.6 1.4 copy-start.7
  511.1 1.4 copy-start.2
  511.7 0.8 copy-start.3
  512.5 19.5 %copy-start.8 = (f32[256,256]{1,0:T(8,128)S(1)}, f32[256,256]{1,0:T(8,128)}, u32[]{:S(2)}) copy-start(f32[256,256]{1,0:T(8,128)} %param.9) | copy-start | bytes 786436
  512.5 20.4 %copy-start.9 = (bf16[96,256]{1,0:T(8,128)(2,1)S(1)}, bf16[96,256]{1,0:T(8,128)(2,1)}, u32[]{:S(2)}) copy-start(bf16[96,256]{1,0:T(8,128)(2,1)} %get-tuple-element.6) | copy-start | bytes 147460
  513.6 291.1 %all-reduce.7.cloned.1.call-start = ((), (), s32[]{:S(2)}) async-start(), calls=%async_computation.8 | async-start | bytes 524288 | tf_op jit(solution)/shard_map/psum | solution.py:45
  534.0 388.2 %all-gather.5.cloned.1.call-start = ((), (), s32[]{:S(2)}) async-start(), calls=%async_computation.9 | async-start | bytes 1585152 | tf_op jit(solution)/shard_map/all_gather | solution.py:51
  922.3 7.9 copy-start.12
  922.3 30.6 %all-to-all-start.1 = ((bf16[4,32,1,24,256]{4,3,1,2,0:T(8,128)(2,1)}), bf16[4,32,1,24,256]{4,3,1,2,0:T(8,128)(2,1)S(1)}, u32[]{:S(2)}, u32[]{:S(2)}) async-start(bf16[4,32,1,24,256]{4,3,1,2,0:T(8,128)(2,1)} %bitcast.47), calls=%async_computation.3 | async-start | bytes 3145728 | tf_op jit(solution)/shard_map/all_to_all | solution.py:53
  952.8 1.1 copy-start.4
  952.8 1.5 copy-start.5
Sparse Core Ops, SparseCore 0:
  10.1 28.0 reduce-scatter.2
  41.5 47.2 all-reduce.8
  93.7 267.9 all-reduce.4
  366.3 112.7 all-gather.2
  513.7 18.2 reduce-scatter.4
  536.8 267.8 all-reduce.6
  809.5 112.7 all-gather.4
where the time goes:
time: 963 us
  waiting for transfers between devices  866 us (90%)
  blocking collectives  42 us (4%)
  matrix products  19.3 us (2%)
  starting transfers between devices  16 us (2%)
  between operations  13.6 us (1%)
    psum x2, waiting for transfers between devices, body(): lax.psum(jnp.dot(local_rows.T, product, precision=high), ('prow', 'pcol'))  542 us
    all_gather x2, waiting for transfers between devices, body(): gathered = lax.all_gather(quarter, 'pcol', axis=0, tiled=True)  229 us
    psum x1, waiting for transfers between devices, from_root(): return lax.psum(jnp.where(mine, x, jnp.zeros_like(x)), axis)  49.5 us
    reduce_scatter x2, waiting for transfers between devices, body(): sums = lax.psum_scatter(term, 'prow', scatter_dimension=0, tiled=True)  45.1 us
    all_gather x2, blocking collectives, body(): col_wide = lax.all_gather(quarter, 'prow', axis=0, tiled=True)  42 us
  transfers between devices with their start and end apart: 9, of which 7 were waited for; matrix products, arithmetic and copies ran while one was open for 1% of the time, Pallas kernels for 0%

commit v1 on v0

v1 whole, which is shorter than its diff:
```python
import functools

import jax
import jax.numpy as jnp
from jax import lax
from jax.experimental import pallas as pl
from jax.experimental.pallas import tpu as pltpu
from jax.sharding import PartitionSpec as P

MESH = pl.DeviceIdType.MESH
HIGH = lax.Precision.HIGHEST
PARTS = (8, 8, 2)
ROWS = 4
F32 = jnp.float32
BF16 = jnp.bfloat16


def dot(lhs, rhs, left=1, right=0, precision=None):
    return lax.dot_general(
        lhs, rhs, (((left,), (right,)), ((), ())), precision=precision, preferred_element_type=F32
    )


def kernel(
    parts,
    a_hbm, v1_hbm, v2_hbm, f1_hbm, f2_hbm,
    out,
    a, v, f, term, rs_buf, s_buf, unit, s, cols, cross, cross_buf, cross_far, at, base, hacc, h_buf, h_send, h_far,
    load, rs_tx, rs_rx, vc_tx, vc_rx, sg_tx, sg_rx, sc_tx, sc_rx, c_tx, c_rx, h_tx, h_rx,
    y_tx, y_rx, z_tx, z_rx, ring_tx, ring_rx,
):
    nz, ny, nh = parts
    depth = nz // ROWS
    half_rows, panel = unit.shape
    width = 2 * half_rows
    p = lax.axis_index("prow")
    q = lax.axis_index("pcol")
    z, y, h = q // (ny * nh), (q // nh) % ny, q % nh
    lo, core = p // 2, p % 2
    mates = (2 * lo + 1 - core, 2 * (1 - lo) + core, 3 - p)

    def at_device(row, zi, yi, hi):
        return {"prow": row, "pcol": (zi * ny + yi) * nh + hi}

    def peer(k):
        return {"prow": mates[k], "pcol": q}

    def remote(src, dst, tx, rx, device):
        return pltpu.make_async_remote_copy(
            src_ref=src, dst_ref=dst, send_sem=tx, recv_sem=rx, device_id=device, device_id_type=MESH
        )

    owner, slab = z // depth, z % depth
    my_slab, my_piece = z // 4, z % 4
    to_z = (slab * 2 + h) * 2 + lo
    stays = (owner == p) & (to_z == z)
    from_z, from_h, from_lo = p * depth + my_slab, my_piece // 2, my_piece % 2

    loads = [
        pltpu.make_async_copy(a_hbm, a, load.at[0]),
        pltpu.make_async_copy(v1_hbm, v.at[0], load.at[1]),
        pltpu.make_async_copy(v2_hbm, v.at[1], load.at[2]),
        pltpu.make_async_copy(f1_hbm, f.at[0], load.at[3]),
        pltpu.make_async_copy(f2_hbm, f.at[1], load.at[4]),
    ]
    for copy in loads:
        copy.start()

    barrier = pltpu.get_barrier_semaphore()

    def greet(device):
        pl.semaphore_signal(barrier, inc=1, device_id=device, device_id_type=MESH)

    for k in range(3):
        greet(peer(k))
    for k in range(1, ny):
        greet(at_device(p, z, (y + k) % ny, h))
    for k in range(1, nz):
        greet(at_device(p, (z + k) % nz, y, h))
    for panel_id in range(2):
        from_p = from_lo * 2 + panel_id

        @pl.when(jnp.logical_not((from_p == p) & (from_z == z) & (from_h == h)))
        def _():
            greet(at_device(from_p, from_z, y, from_h))

    for copy in loads[:3]:
        copy.wait()
    rows = v.shape[1] * v.shape[2] * v.shape[3] * v.shape[4]
    for panel_id in range(2):
        part = dot(a[...], v[panel_id].reshape(rows, panel), 0, 0)
        term[panel_id] = part.reshape(2, half_rows, panel)

    expected = 3 + (ny - 1) + (nz - 1) + 2 - jnp.where(stays, 1, 0)
    pl.semaphore_wait(barrier, expected)

    scattered = []
    for k in (2, 1, 0):
        mate = mates[k]
        copy = remote(term.at[mate % 2, mate // 2], rs_buf.at[k], rs_tx.at[k], rs_rx.at[k], peer(k))
        copy.start()
        scattered.append(copy)

    mine = v.at[:, slab, y, pl.ds(2 * h, 2)]
    col_copies = [remote(mine, cols, vc_tx.at[k], vc_rx, peer(k)) for k in range(3)]
    col_local = pltpu.make_async_copy(mine, cols, vc_rx)

    @pl.when(owner == p)
    def _():
        for copy in col_copies:
            copy.start()
        col_local.start()

    cross[...] = dot(v[0].reshape(rows, panel), v[1].reshape(rows, panel), 0, 0)
    cross_near = remote(cross, cross_buf, c_tx.at[0], c_rx.at[0], peer(0))
    cross_near.start()

    for copy in scattered:
        copy.wait_recv()
    total = term[core, lo] + rs_buf[0] + rs_buf[1] + rs_buf[2]
    s_buf[core, lo] = total
    unit[...] = total.astype(BF16)

    landing = s.at[core, slab, y, h * 2 + lo]
    far_unit = remote(unit, landing, sc_tx.at[0], sc_rx.at[core], at_device(owner, to_z, y, 1 - h))
    near_unit = remote(unit, landing, sc_tx.at[1], sc_rx.at[core], at_device(owner, to_z, y, h))
    near_local = pltpu.make_async_copy(unit, landing, sc_rx.at[core])
    far_unit.start()

    @pl.when(stays)
    def _():
        near_local.start()

    @pl.when(jnp.logical_not(stays))
    def _():
        near_unit.start()

    groups = []
    for k in range(3):
        copy = remote(s_buf.at[core, lo], s_buf.at[core, lo], sg_tx.at[k], sg_rx.at[k], peer(k))
        copy.start()
        groups.append(copy)

    gathers = []
    slot = s.at[0, my_slab, y, my_piece]
    pltpu.make_async_copy(slot, slot, sc_rx.at[0]).wait()
    for k in range(1, ny):
        copy = remote(slot, slot, y_tx.at[k], y_rx.at[k], at_device(p, z, (y + k) % ny, h))
        copy.start()
        gathers.append(copy)
    slot = s.at[1, my_slab, y, my_piece]
    pltpu.make_async_copy(slot, slot, sc_rx.at[1]).wait()
    for k in range(1, nz):
        copy = remote(slot, slot, z_tx.at[k], z_rx.at[k], at_device(p, (z + k) % nz, y, h))
        copy.start()
        gathers.append(copy)

    cross_near.wait()
    cross_buf[...] = cross_buf[...] + cross[...]
    cross_twin = remote(cross_buf, cross_far, c_tx.at[1], c_rx.at[1], peer(1))
    cross_twin.start()
    base[...] = a[...].astype(F32).reshape(base.shape)
    hacc[...] = jnp.zeros_like(hacc)
    loads[3].wait()
    loads[4].wait()
    pltpu.make_async_copy(mine, cols, vc_rx).wait()
    second = dot(f[1], cols[1].reshape(width, panel).astype(F32), 1, 1, HIGH)
    at[1] = second.astype(BF16)
    first = dot(f[0], cols[0].reshape(width, panel).astype(F32), 1, 1, HIGH)

    def block(ring, place, part):
        if ring == 0:
            return 0, place // 4, pl.ds(part * (ny // 2), ny // 2), place % 4
        if depth > 1:
            return 1, pl.ds(part * (depth // 2), depth // 2), place, slice(None)
        return 1, 0, place, pl.ds(part * 2, 2)

    def ring_copy(ring, way, step, part):
        count, here = ((nz, z), (ny, y))[ring]
        sign = 1 - 2 * way
        place = (here - sign * (step - 1) + count) % count
        ahead = (here + sign + count) % count
        device = at_device(p, ahead, y, h) if ring == 0 else at_device(p, z, ahead, h)
        index = 2 * (step - 1) + (part if step < count // 2 else 0)
        where = s.at[block(ring, place, part)]
        return remote(where, where, ring_tx.at[ring, way, index], ring_rx.at[ring, way, index], device)

    def sent(ring, way, step, part):
        count = (nz, ny)[ring]
        return step < count // 2 or (step == count // 2 and part == way)

    for k in range(1, ny):
        where = s.at[0, my_slab, (y - k + ny) % ny, my_piece]
        remote(where, where, y_tx.at[k], y_rx.at[k], peer(0)).wait_recv()
    started = []
    for part in range(2):
        for way in range(2):
            if sent(0, way, 1, part):
                copy = ring_copy(0, way, 1, part)
                copy.start()
                started.append(copy)
    for k in range(1, nz):
        source = (z - k + nz) % nz
        where = s.at[1, source // 4, y, source % 4]
        remote(where, where, z_tx.at[k], z_rx.at[k], peer(0)).wait_recv()
    for part in range(2):
        for way in range(2):
            if sent(1, way, 1, part):
                copy = ring_copy(1, way, 1, part)
                copy.start()
                started.append(copy)

    cross_twin.wait()
    cross[...] = cross_buf[...] + cross_far[...]
    first = first - dot(f[0], dot(cross[...], second, 1, 0, HIGH), 1, 0, HIGH)
    at[0] = first.astype(BF16)

    def apply(ring, place, part):
        index = block(ring, place, part)
        tail = index[1:]
        values = s[index]
        lead = values.shape[:-1]
        count = values.size // panel
        piece = dot(values.reshape(count, panel), at[ring])
        base[tail] = base[tail] - piece.reshape(*lead, width)
        piece = piece.astype(BF16)
        for panel_id in range(2):
            vectors = v[(panel_id, *tail)].reshape(count, panel)
            hacc[panel_id] = hacc[panel_id] + dot(piece, vectors, 0, 0)

    for part in range(2):
        apply(0, z, part)
        apply(1, y, part)

    for step in range(1, max(nz, ny) // 2 + 1):
        for part in range(2):
            for ring in range(2):
                for way in range(2):
                    if not sent(ring, way, step, part):
                        continue
                    count, here = ((nz, z), (ny, y))[ring]
                    sign = 1 - 2 * way
                    place = (here - sign * step + count) % count
                    index = 2 * (step - 1) + (part if step < count // 2 else 0)
                    where = s.at[block(ring, place, part)]
                    remote(
                        where, where, ring_tx.at[ring, way, index], ring_rx.at[ring, way, index], peer(0)
                    ).wait_recv()
                    if sent(ring, way, step + 1, part):
                        copy = ring_copy(ring, way, step + 1, part)
                        copy.start()
                        started.append(copy)
                    apply(ring, place, part)

    near = remote(hacc, h_buf, h_tx.at[0], h_rx.at[0], peer(0))
    near.start()
    for copy in groups:
        copy.wait_send()
    for k in range(3):
        mate = mates[k]
        where = s_buf.at[mate % 2, mate // 2]
        remote(where, where, sg_tx.at[k], sg_rx.at[k], peer(k)).wait_recv()
    near.wait()
    chip = hacc[...] + h_buf[...]
    h_send[...] = chip.astype(BF16)
    twin = remote(h_send, h_far, h_tx.at[1], h_rx.at[1], peer(1))
    twin.start()
    twin.wait()
    rest = s_buf[...].reshape(2, width, panel) - chip - h_far[...].astype(F32)
    left_one = dot(rest[0], f[0], 1, 0, HIGH)
    left_two = dot(rest[1] - dot(left_one, cross[...], 1, 0, HIGH), f[1], 1, 0, HIGH)
    left_one = left_one.astype(BF16)
    left_two = left_two.astype(BF16)

    for slab_id in range(v.shape[1]):
        for column in range(ny):
            count = 4 * half_rows
            update = dot(v[0, slab_id, column].reshape(count, panel), left_one, 1, 1)
            update = update + dot(v[1, slab_id, column].reshape(count, panel), left_two, 1, 1)
            result = base[slab_id, column].reshape(count, width) - update
            out[pl.ds((slab_id * ny + column) * count, count)] = result.astype(BF16)

    for copy in scattered + gathers + started:
        copy.wait_send()
    far_unit.wait_send()

    @pl.when(jnp.logical_not(stays))
    def _():
        near_unit.wait_send()

    @pl.when(owner == p)
    def _():
        for copy in col_copies:
            copy.wait_send()


def body(parts, matrix, vectors_one, factor_one, vectors_two, factor_two):
    nz, ny, nh = parts
    depth = nz // ROWS
    rows, width = matrix.shape
    panel = factor_one.shape[0]
    half = width // 2
    grid = (depth, ny, 4, half)
    hbm = pl.BlockSpec(memory_space=pl.ANY)
    dma = pltpu.SemaphoreType.DMA
    most = max(nz, ny)
    flops = 2 * rows * width * panel * 10
    return pl.pallas_call(
        functools.partial(kernel, parts),
        out_shape=jax.ShapeDtypeStruct((rows, width), BF16),
        in_specs=[hbm] * 5,
        out_specs=pl.BlockSpec(memory_space=pltpu.VMEM),
        scratch_shapes=[
            pltpu.VMEM((rows, width), BF16),
            pltpu.VMEM((2, *grid, panel), BF16),
            pltpu.VMEM((2, panel, panel), F32),
            pltpu.VMEM((2, 2, half, panel), F32),
            pltpu.VMEM((3, half, panel), F32),
            pltpu.VMEM((2, 2, half, panel), F32),
            pltpu.VMEM((half, panel), BF16),
            pltpu.VMEM((2, *grid, panel), BF16),
            pltpu.VMEM((2, 2, half, panel), BF16),
            pltpu.VMEM((panel, panel), F32),
            pltpu.VMEM((panel, panel), F32),
            pltpu.VMEM((panel, panel), F32),
            pltpu.VMEM((2, panel, width), BF16),
            pltpu.VMEM((*grid, width), F32),
            pltpu.VMEM((2, width, panel), F32),
            pltpu.VMEM((2, width, panel), F32),
            pltpu.VMEM((2, width, panel), BF16),
            pltpu.VMEM((2, width, panel), BF16),
            dma((5,)),
            dma((3,)),
            dma((3,)),
            dma((3,)),
            dma,
            dma((3,)),
            dma((3,)),
            dma((2,)),
            dma((2,)),
            dma((2,)),
            dma((2,)),
            dma((2,)),
            dma((2,)),
            dma((ny,)),
            dma((ny,)),
            dma((nz,)),
            dma((nz,)),
            dma((2, 2, most)),
            dma((2, 2, most)),
        ],
        compiler_params=pltpu.CompilerParams(
            collective_id=0, has_side_effects=True, vmem_limit_bytes=40 * 1024 * 1024
        ),
        cost_estimate=pl.CostEstimate(flops=flops, bytes_accessed=4 * rows * panel, transcendentals=0),
    )(
        matrix,
        vectors_one.reshape(*grid, panel),
        vectors_two.reshape(*grid, panel),
        factor_one,
        factor_two,
    )


def build(mesh, parts):
    placed = (P("prow", "pcol"), P("prow", None), P(), P("prow", None), P())
    return jax.shard_map(
        functools.partial(body, parts), mesh=mesh, in_specs=placed, out_specs=P("prow", "pcol"), check_vma=False
    )


def solution(mesh):
    return build(mesh, PARTS)
```

time: 963 us -> 68.3 us (0.07)
  waiting for transfers between devices: 866 us -> 0 us
  Pallas kernels: 0 us -> 60.5 us
  blocking collectives: 42 us -> 0 us
  matrix products: 19.3 us -> 0 us
  starting transfers between devices: 16 us -> 0 us
  between operations: 13.6 us -> 0.03 us
    psum x3 -> x0, waiting for transfers between devices: 591 us -> none  [the longest x2 542 us: body(): lax.psum(jnp.dot(local_rows.T, product, precision=high), ('prow', 'pcol'))]
    all_gather x2 -> x0, waiting for transfers between devices: 229 us -> none  [body(): gathered = lax.all_gather(quarter, 'pcol', axis=0, tiled=True)]
    pallas_call x0 -> x1, Pallas kernels: none -> 60.5 us  [body(): pl.pallas_call(functools.partial(kernel, parts), out_shape=jax.ShapeDtype...]
    reduce_scatter x2 -> x0, waiting for transfers between devices: 45.1 us -> none  [body(): sums = lax.psum_scatter(term, 'prow', scatter_dimension=0, tiled=True)]
    all_gather x2 -> x0, blocking collectives: 42 us -> none  [body(): col_wide = lax.all_gather(quarter, 'prow', axis=0, tiled=True)]
    dot_general x14 -> x0, matrix products: 19.3 us -> none  [the longest x2 3.77 us: body(): lax.dot_general(current, vectors, (((0,), (0,)), ((), ())), preferred_ele...]
    all_to_all x2 -> x0, starting transfers between devices: 15.8 us -> none  [body(): lax.all_to_all(sectioned, 'prow', split_axis=0, concat_axis=2, tiled=True)]
  transfers between devices with their start and end apart: 9 -> 0, of which waited for: 7 -> 0; matrix products, arithmetic and copies ran while one was open for 1% -> 0% of each run, Pallas kernels for 0% -> 0%
where the time goes in v1:
time: 68.3 us; the launch traced here: 67.7 us
  Pallas kernels  60.5 us (89%)
  local copies, waits for them, and re-layouts  7.24 us (11%)
    pallas_call x1, Pallas kernels, body(): pl.pallas_call(functools.partial(kernel, parts), out_shape=jax.ShapeDtype...  60.5 us
    unnamed x9, local copies, waits for them, and re-layouts  6.15 us

profile of v1, /device:TPU:1, one launch (start us, length us, event | category | flops | bytes accessed | tf_op | source)
XLA Modules:
  0.0 67.7 jit_solution(3002929641496744694)
XLA Ops:
  0.0 1.4 %copy.6.a_hbm = bf16[3072,96]{1,0:T(8,128)(2,1)S(1)} copy(bf16[3072,96]{0,1:T(8,128)(2,1)} %param.5) | data formatting | bytes 1179648 | tf_op args[0]
  1.4 0.0 copy-start
  1.5 1.4 %copy-done = bf16[3072,256]{1,0:T(8,128)(2,1)S(1)} copy-done((bf16[3072,256]{1,0:T(8,128)(2,1)S(1)}, bf16[3072,256]{1,0:T(8,128)(2,1)}, u32[]{:S(2)}) %copy-start) | copy-done | bytes 1572888
  2.9 0.0 copy-start.1
  2.9 1.4 %copy-done.1 = bf16[3072,256]{1,0:T(8,128)(2,1)S(1)} copy-done((bf16[3072,256]{1,0:T(8,128)(2,1)S(1)}, bf16[3072,256]{1,0:T(8,128)(2,1)}, u32[]{:S(2)}) %copy-start.1) | copy-done | bytes 1572888
  4.3 0.0 copy-start.2
  4.3 0.9 %copy-done.2 = f32[256,256]{1,0:T(8,128)S(1)} copy-done((f32[256,256]{1,0:T(8,128)S(1)}, f32[256,256]{1,0:T(8,128)}, u32[]{:S(2)}) %copy-start.2) | copy-done | bytes 262168
  5.2 0.0 copy-start.3
  5.2 0.9 %copy-done.3 = f32[256,256]{1,0:T(8,128)S(1)} copy-done((f32[256,256]{1,0:T(8,128)S(1)}, f32[256,256]{1,0:T(8,128)}, u32[]{:S(2)}) %copy-start.3) | copy-done | bytes 262168
  6.2 60.5 %shard_map.55 = bf16[3072,96]{1,0:T(8,128)(2,1)S(1)} custom-call(bf16[3072,96]{1,0:T(8,128)(2,1)S(1)} %copy.6.a_hbm, bf16[2,8,4,48,256]{4,3,2,1,0:T(8,128)(2,1)S(1)} %bitcast.2, bf16[2,8,4,48,256]{4,3,2,1,0:T(8,128)(2,1)S(1)} %bitcast.3, f32[256,256]{1,0:T(8,128)S(1)} %copy-done.2, f32[256,256]{1,0:T(8,128)S(1)} %copy-done.3), custom_call_target="tpu_custom_call" | custom-call | flops 1509949440 | bytes 3145728 | tf_op jit(solution)/shard_map/pallas_call | solution.py:308
  66.6 1.1 %copy.7 = bf16[3072,96]{0,1:T(8,128)(2,1)} copy(bf16[3072,96]{1,0:T(8,128)(2,1)S(1)} %shard_map.55) | data formatting | bytes 1179648 | tf_op jit(solution)/shard_map/pallas_call | solution.py:308
Async XLA Ops:
  1.4 1.4 %copy-start = (bf16[3072,256]{1,0:T(8,128)(2,1)S(1)}, bf16[3072,256]{1,0:T(8,128)(2,1)}, u32[]{:S(2)}) copy-start(bf16[3072,256]{1,0:T(8,128)(2,1)} %param.6) | copy-start | bytes 4718596
  2.9 1.4 %copy-start.1 = (bf16[3072,256]{1,0:T(8,128)(2,1)S(1)}, bf16[3072,256]{1,0:T(8,128)(2,1)}, u32[]{:S(2)}) copy-start(bf16[3072,256]{1,0:T(8,128)(2,1)} %param.8) | copy-start | bytes 4718596
  4.3 0.9 %copy-start.2 = (f32[256,256]{1,0:T(8,128)S(1)}, f32[256,256]{1,0:T(8,128)}, u32[]{:S(2)}) copy-start(f32[256,256]{1,0:T(8,128)} %f1_hbm.1) | copy-start | bytes 786436
  5.2 0.9 %copy-start.3 = (f32[256,256]{1,0:T(8,128)S(1)}, f32[256,256]{1,0:T(8,128)}, u32[]{:S(2)}) copy-start(f32[256,256]{1,0:T(8,128)} %f2_hbm.1) | copy-start | bytes 786436

commit v2 on v1

v2 whole, which is shorter than its diff:
```python
import functools

import jax
import jax.numpy as jnp
from jax import lax
from jax.experimental import pallas as pl
from jax.experimental.pallas import tpu as pltpu
from jax.sharding import PartitionSpec as P

MESH = pl.DeviceIdType.MESH
HIGH = lax.Precision.HIGHEST
PARTS = (8, 8, 2)
ROWS = 4
F32 = jnp.float32
BF16 = jnp.bfloat16


def dot(lhs, rhs, left=1, right=0, precision=None):
    return lax.dot_general(
        lhs, rhs, (((left,), (right,)), ((), ())), precision=precision, preferred_element_type=F32
    )


def kernel(
    parts,
    a_hbm, v1_hbm, v2_hbm, f1_hbm, f2_hbm,
    out,
    a, v, f, term, rs_buf, s_buf, unit, s, cols, cross, cross_buf, cross_far, at, base, hacc, h_buf, h_send, h_far,
    load, f_load, rs_tx, rs_rx, vc_tx, vc_rx, sg_tx, sg_rx, sc_tx, sc_rx, c_tx, c_rx, h_tx, h_rx,
    first_tx, first_rx, ring_tx, ring_rx,
):
    nz, ny, nh = parts
    depth = nz // ROWS
    half_rows, panel = unit.shape
    width = 2 * half_rows
    run = 4 * half_rows
    p = lax.axis_index("prow")
    q = lax.axis_index("pcol")
    z, y, h = q // (ny * nh), (q // nh) % ny, q % nh
    lo, core = p // 2, p % 2
    mates = (2 * lo + 1 - core, 2 * (1 - lo) + core, 3 - p)

    def at_device(row, zi, yi, hi):
        return {"prow": row, "pcol": (zi * ny + yi) * nh + hi}

    def peer(k):
        return {"prow": mates[k], "pcol": q}

    def remote(src, dst, tx, rx, device):
        return pltpu.make_async_remote_copy(
            src_ref=src, dst_ref=dst, send_sem=tx, recv_sem=rx, device_id=device, device_id_type=MESH
        )

    later = []

    def send(copy):
        copy.start()
        later.append(copy.wait_send)

    owner, slab = z // depth, z % depth
    counts, heres = (nz, ny), (z, y)

    def along(ring, place):
        return at_device(p, place, y, h) if ring == 0 else at_device(p, z, place, h)

    number = (slab * 4) + 2 * h + lo
    to = jnp.where(core == 0, y, number), jnp.where(core == 0, number, y)
    stays = (owner == p) & (to[0] == z) & (to[1] == y)

    def origin(k):
        place, unit_number = ((z, y), (y, z))[k]
        piece = unit_number % 4
        return 2 * (piece % 2) + k, p * depth + unit_number // 4, place, piece // 2

    halves = [(k, part) for part in range(depth) for k in range(2)]
    loads = [pltpu.make_async_copy(a_hbm, a, load.at[0])]
    for place, (k, part) in enumerate(halves):
        loads.append(pltpu.make_async_copy((v1_hbm, v2_hbm)[k].at[part], v.at[k, part], load.at[1 + place]))
    for copy in loads:
        copy.start()
    factors = [pltpu.make_async_copy((f1_hbm, f2_hbm)[k], f.at[k], f_load.at[k]) for k in range(2)]
    for copy in factors:
        copy.start()

    barrier = pltpu.get_barrier_semaphore()

    def greet(device):
        pl.semaphore_signal(barrier, inc=1, device_id=device, device_id_type=MESH)

    for k in range(3):
        greet(peer(k))
    for ring in range(2):
        for k in range(1, counts[ring]):
            greet(along(ring, (heres[ring] + k) % counts[ring]))
    for k in range(2):
        from_p, from_z, from_y, from_h = origin(k)

        @pl.when(jnp.logical_not((from_p == p) & (from_z == z) & (from_y == y) & (from_h == h)))
        def _():
            greet(at_device(from_p, from_z, from_y, from_h))

    stretch = ny * run
    sums = [None, None]
    loads[0].wait()
    for place, (k, part) in enumerate(halves):
        loads[1 + place].wait()
        more = dot(a[:, part * stretch : (part + 1) * stretch], v[k, part].reshape(stretch, panel))
        sums[k] = more if sums[k] is None else sums[k] + more
    for k in range(2):
        term[k] = sums[k].reshape(2, half_rows, panel)

    pl.semaphore_wait(barrier, 3 + (ny - 1) + (nz - 1) + 2 - jnp.where(stays, 1, 0))

    scattered = []
    for k in (2, 1, 0):
        mate = mates[k]
        copy = remote(term.at[mate % 2, mate // 2], rs_buf.at[k], rs_tx.at[k], rs_rx.at[k], peer(k))
        send(copy)
        scattered.append(copy)

    rows = depth * stretch
    cross[...] = dot(v[0].reshape(rows, panel), v[1].reshape(rows, panel), 0, 0)

    for copy in scattered:
        copy.wait_recv()
    total = term[core, lo] + rs_buf[0] + rs_buf[1] + rs_buf[2]
    unit[...] = total.astype(BF16)
    s_buf[core, lo] = total

    landing = s.at[core, slab, y, pl.ds((2 * h + lo) * half_rows, half_rows)]
    far_unit = remote(unit, landing, sc_tx.at[0], sc_rx.at[core], at_device(owner, to[0], to[1], 1 - h))
    near_unit = remote(unit, landing, sc_tx.at[1], sc_rx.at[core], at_device(owner, to[0], to[1], h))
    near_local = pltpu.make_async_copy(unit, landing, sc_rx.at[core])
    send(far_unit)

    @pl.when(stays)
    def _():
        near_local.start()

    @pl.when(jnp.logical_not(stays))
    def _():
        near_unit.start()

    def near_sent():
        @pl.when(jnp.logical_not(stays))
        def _():
            near_unit.wait_send()

    later.append(near_sent)

    def first_slot(k, unit_number):
        piece = pl.multiple_of(unit_number % 4 * half_rows, half_rows)
        return s.at[k, unit_number // 4, heres[k], pl.ds(piece, half_rows)]

    for k in range(2):
        slot = first_slot(k, heres[1 - k])
        pltpu.make_async_copy(slot, slot, sc_rx.at[k]).wait()
        count = counts[1 - k]
        for j in range(1, count):
            send(remote(slot, slot, first_tx.at[k, j], first_rx.at[k, j], along(1 - k, (heres[1 - k] + j) % count)))

    for k in range(3):
        send(remote(s_buf.at[core, lo], s_buf.at[core, lo], sg_tx.at[k], sg_rx.at[k], peer(k)))
    mine = v.at[:, slab, y, pl.ds(pl.multiple_of(2 * h * half_rows, half_rows), width)]
    col_copies = [remote(mine, cols, vc_tx.at[k], vc_rx, peer(k)) for k in range(3)]
    col_local = pltpu.make_async_copy(mine, cols, vc_rx)

    @pl.when(owner == p)
    def _():
        for copy in col_copies:
            copy.start()
        col_local.start()

    def cols_sent():
        @pl.when(owner == p)
        def _():
            for copy in col_copies:
                copy.wait_send()

    later.append(cols_sent)
    cross_near = remote(cross, cross_buf, c_tx.at[0], c_rx.at[0], peer(0))
    cross_near.start()
    hacc[...] = jnp.zeros_like(hacc)
    base[...] = jnp.zeros_like(base)
    cross_near.wait()
    cross_buf[...] = cross_buf[...] + cross[...]
    cross_twin = remote(cross_buf, cross_far, c_tx.at[1], c_rx.at[1], peer(1))
    cross_twin.start()
    for copy in factors:
        copy.wait()

    def sums_here():
        for k in range(3):
            mate = mates[k]
            where = s_buf.at[mate % 2, mate // 2]
            remote(where, where, sg_tx.at[k], sg_rx.at[k], peer(k)).wait_recv()

    def firsts_here(k):
        count = counts[1 - k]
        for j in range(1, count):
            where = first_slot(k, (heres[1 - k] - j + count) % count)
            remote(where, where, first_tx.at[k, j], first_rx.at[k, j], peer(0)).wait_recv()

    def cols_here():
        pltpu.make_async_copy(mine, cols, vc_rx).wait()


    def block(ring, place, part):
        if depth > 1:
            return s.at[ring, part, place]
        return s.at[ring, 0, place, pl.ds(part * (run // 2), run // 2)]

    def sent(ring, way, step, part):
        half_way = counts[ring] // 2
        return step < half_way or (step == half_way and part == way)

    def ring_copy(ring, way, step, part, receiving=False):
        count, here, sign = counts[ring], heres[ring], 1 - 2 * way
        place = (here - sign * (step if receiving else step - 1) + count) % count
        index = 2 * (step - 1) + (part if step < count // 2 else 0)
        where = block(ring, place, part)
        sems = ring_tx.at[ring, way, index], ring_rx.at[ring, way, index]
        return remote(where, where, *sems, along(ring, (here + sign + count) % count))

    for ring in range(2):
        firsts_here(ring)
        for part in range(2):
            for way in range(2):
                if sent(ring, way, 1, part):
                    send(ring_copy(ring, way, 1, part))

    cols_here()
    second = dot(cols[1].astype(F32), f[1], 1, 1, HIGH)
    at[1] = second.astype(BF16)
    cross_twin.wait()
    cross[...] = cross_buf[...] + cross_far[...]
    first = dot(cols[0].astype(F32) - dot(second, cross[...], 1, 1, HIGH), f[0], 1, 1, HIGH)
    at[0] = first.astype(BF16)

    def apply(ring, place, part):
        if depth > 1:
            tail = (part, place)
        else:
            tail = (0, place, slice(part * (run // 2), (part + 1) * (run // 2)))
        piece = dot(at[ring], s[(ring, *tail)], 1, 1)
        if depth > 1:
            base[part, place] = base[part, place] + piece
        else:
            base[0, place, :, tail[2]] = base[0, place, :, tail[2]] + piece
        piece = piece.astype(BF16)
        for k in range(2):
            hacc[k] = hacc[k] + dot(piece, v[(k, *tail)])

    for part in range(2):
        for ring in range(2):
            apply(ring, heres[ring], part)

    for step in range(1, max(nz, ny) // 2 + 1):
        for part in range(2):
            for ring in range(2):
                for way in range(2):
                    if not sent(ring, way, step, part):
                        continue
                    ring_copy(ring, way, step, part, receiving=True).wait_recv()
                    if sent(ring, way, step + 1, part):
                        send(ring_copy(ring, way, step + 1, part))
                    count, here, sign = counts[ring], heres[ring], 1 - 2 * way
                    apply(ring, (here - sign * step + count) % count, part)

    sums_here()
    near = remote(hacc, h_buf, h_tx.at[0], h_rx.at[0], peer(0))
    near.start()
    near.wait()
    chip = hacc[...] + h_buf[...]
    h_send[...] = chip.astype(BF16)
    twin = remote(h_send, h_far, h_tx.at[1], h_rx.at[1], peer(1))
    twin.start()
    rest = s_buf[...].reshape(2, width, panel) - chip
    twin.wait()
    rest = rest - h_far[...].astype(F32)
    left_one = dot(rest[0], f[0], 1, 0, HIGH)
    left_two = dot(rest[1] - dot(left_one, cross[...], 1, 0, HIGH), f[1], 1, 0, HIGH)
    left = left_one.astype(BF16), left_two.astype(BF16)

    for part in range(depth):
        for place in range(0, ny, 2):
            spot = slice((part * ny + place) * run, (part * ny + place + 2) * run)
            pair = slice(place, place + 2)
            update = jnp.concatenate([base[part, place], base[part, place + 1]], axis=1)
            for k in range(2):
                update = update + dot(left[k], v[k, part, pair].reshape(2 * run, panel), 1, 1)
            out[:, spot] = (a[:, spot].astype(F32) - update).astype(BF16)

    for wait in later:
        wait()


def body(parts, matrix, vectors_one, factor_one, vectors_two, factor_two):
    nz, ny, nh = parts
    depth = nz // ROWS
    rows, width = matrix.shape
    panel = factor_one.shape[0]
    half = width // 2
    grid = (depth, ny, 4 * half)
    hbm = pl.BlockSpec(memory_space=pltpu.HBM)
    dma = pltpu.SemaphoreType.DMA
    most = max(nz, ny)
    flops = 2 * rows * width * panel * 10
    result = pl.pallas_call(
        functools.partial(kernel, parts),
        out_shape=jax.ShapeDtypeStruct((width, rows), BF16),
        in_specs=[hbm] * 5,
        out_specs=pl.BlockSpec(memory_space=pltpu.VMEM),
        scratch_shapes=[
            pltpu.VMEM((width, rows), BF16),
            pltpu.VMEM((2, *grid, panel), BF16),
            pltpu.VMEM((2, panel, panel), F32),
            pltpu.VMEM((2, 2, half, panel), F32),
            pltpu.VMEM((3, half, panel), F32),
            pltpu.VMEM((2, 2, half, panel), F32),
            pltpu.VMEM((half, panel), BF16),
            pltpu.VMEM((2, *grid, panel), BF16),
            pltpu.VMEM((2, width, panel), BF16),
            pltpu.VMEM((panel, panel), F32),
            pltpu.VMEM((panel, panel), F32),
            pltpu.VMEM((panel, panel), F32),
            pltpu.VMEM((2, width, panel), BF16),
            pltpu.VMEM((depth, ny, width, 4 * half), F32),
            pltpu.VMEM((2, width, panel), F32),
            pltpu.VMEM((2, width, panel), F32),
            pltpu.VMEM((2, width, panel), BF16),
            pltpu.VMEM((2, width, panel), BF16),
            dma((1 + 2 * depth,)),
            dma((2,)),
            dma((3,)),
            dma((3,)),
            dma((3,)),
            dma,
            dma((3,)),
            dma((3,)),
            dma((2,)),
            dma((2,)),
            dma((2,)),
            dma((2,)),
            dma((2,)),
            dma((2,)),
            dma((2, most)),
            dma((2, most)),
            dma((2, 2, most)),
            dma((2, 2, most)),
        ],
        compiler_params=pltpu.CompilerParams(
            collective_id=0, has_side_effects=True, vmem_limit_bytes=56 * 1024 * 1024
        ),
        cost_estimate=pl.CostEstimate(flops=flops, bytes_accessed=4 * rows * panel, transcendentals=0),
    )(matrix.T, vectors_one.reshape(*grid, panel), vectors_two.reshape(*grid, panel), factor_one, factor_two)
    return result.T


def build(mesh, parts):
    placed = (P("prow", "pcol"), P("prow", None), P(), P("prow", None), P())
    return jax.shard_map(
        functools.partial(body, parts), mesh=mesh, in_specs=placed, out_specs=P("prow", "pcol"), check_vma=False
    )


def solution(mesh):
    return build(mesh, PARTS)
```

time: 68.3 us -> 67.1 us (0.982)
  local copies, waits for them, and re-layouts: 7.24 us -> 1.92 us
  Pallas kernels: 60.5 us -> 65 us
    pallas_call x1, Pallas kernels: 60.5 us -> 65 us  [body(): pl.pallas_call(functools.partial(kernel, parts), out_shape=jax.ShapeDtype...]
    unnamed x9 -> x1, local copies, waits for them, and re-layouts: 6.15 us -> 1.92 us
    pallas_call x1 -> x0, local copies, waits for them, and re-layouts: 1.09 us -> none  [body(): pl.pallas_call(functools.partial(kernel, parts), out_shape=jax.ShapeDtype...]
where the time goes in v2:
time: 67.1 us; the launch traced here: 67 us
  Pallas kernels  65 us (97%)
  local copies, waits for them, and re-layouts  1.92 us (3%)
    pallas_call x1, Pallas kernels, body(): pl.pallas_call(functools.partial(kernel, parts), out_shape=jax.ShapeDtype...  65 us
    unnamed x1, local copies, waits for them, and re-layouts  1.92 us

profile of v2, /device:TPU:1, one launch (start us, length us, event | category | flops | bytes accessed | tf_op | source)
XLA Modules:
  0.0 67.0 jit_solution(12105403275929966659)
XLA Ops:
  0.0 65.0 %shard_map.55 = bf16[96,3072]{1,0:T(8,128)(2,1)} custom-call(bf16[96,3072]{1,0:T(8,128)(2,1)} %bitcast.7, bf16[2,8,192,256]{3,2,1,0:T(8,128)(2,1)} %bitcast.5, bf16[2,8,192,256]{3,2,1,0:T(8,128)(2,1)} %bitcast.6, f32[256,256]{1,0:T(8,128)} %f1_hbm.1, f32[256,256]{1,0:T(8,128)} %f2_hbm.1), custom_call_target="tpu_custom_call" | custom-call | flops 1509949440 | bytes 3145728 | tf_op jit(solution)/shard_map/pallas_call | solution.py:309
  65.1 1.9 %copy.7 = bf16[3072,96]{0,1:T(8,128)(2,1)} copy(bf16[3072,96]{0,1:T(8,128)(2,1)} %bitcast.4) | data formatting | bytes 1179648

commit v3 on v2

--- a/solution.py
+++ b/solution.py
@@ -63,14 +63,9 @@
     def along(ring, place):
         return at_device(p, place, y, h) if ring == 0 else at_device(p, z, place, h)
 
-    number = (slab * 4) + 2 * h + lo
-    to = jnp.where(core == 0, y, number), jnp.where(core == 0, number, y)
-    stays = (owner == p) & (to[0] == z) & (to[1] == y)
-
-    def origin(k):
-        place, unit_number = ((z, y), (y, z))[k]
-        piece = unit_number % 4
-        return 2 * (piece % 2) + k, p * depth + unit_number // 4, place, piece // 2
+    number = slab * 4 + 2 * h + lo
+    stays = (owner == p) & (number == z)
+    from_z, from_h, from_lo = p * depth + z // 4, z % 4 // 2, z % 2
 
     halves = [(k, part) for part in range(depth) for k in range(2)]
     loads = [pltpu.make_async_copy(a_hbm, a, load.at[0])]
@@ -93,11 +88,11 @@
         for k in range(1, counts[ring]):
             greet(along(ring, (heres[ring] + k) % counts[ring]))
     for k in range(2):
-        from_p, from_z, from_y, from_h = origin(k)
-
-        @pl.when(jnp.logical_not((from_p == p) & (from_z == z) & (from_y == y) & (from_h == h)))
+        from_p = 2 * from_lo + k
+
+        @pl.when(jnp.logical_not((from_p == p) & (from_z == z) & (from_h == h)))
         def _():
-            greet(at_device(from_p, from_z, from_y, from_h))
+            greet(at_device(from_p, from_z, y, from_h))
 
     stretch = ny * run
     sums = [None, None]
@@ -120,16 +115,17 @@
 
     rows = depth * stretch
     cross[...] = dot(v[0].reshape(rows, panel), v[1].reshape(rows, panel), 0, 0)
+    cross_near = remote(cross, cross_buf, c_tx.at[0], c_rx.at[0], peer(0))
+    cross_near.start()
 
     for copy in scattered:
         copy.wait_recv()
     total = term[core, lo] + rs_buf[0] + rs_buf[1] + rs_buf[2]
     unit[...] = total.astype(BF16)
-    s_buf[core, lo] = total
 
     landing = s.at[core, slab, y, pl.ds((2 * h + lo) * half_rows, half_rows)]
-    far_unit = remote(unit, landing, sc_tx.at[0], sc_rx.at[core], at_device(owner, to[0], to[1], 1 - h))
-    near_unit = remote(unit, landing, sc_tx.at[1], sc_rx.at[core], at_device(owner, to[0], to[1], h))
+    far_unit = remote(unit, landing, sc_tx.at[0], sc_rx.at[core], at_device(owner, number, y, 1 - h))
+    near_unit = remote(unit, landing, sc_tx.at[1], sc_rx.at[core], at_device(owner, number, y, h))
     near_local = pltpu.make_async_copy(unit, landing, sc_rx.at[core])
     send(far_unit)
 
@@ -148,16 +144,23 @@
 
     later.append(near_sent)
 
-    def first_slot(k, unit_number):
-        piece = pl.multiple_of(unit_number % 4 * half_rows, half_rows)
-        return s.at[k, unit_number // 4, heres[k], pl.ds(piece, half_rows)]
-
-    for k in range(2):
-        slot = first_slot(k, heres[1 - k])
-        pltpu.make_async_copy(slot, slot, sc_rx.at[k]).wait()
-        count = counts[1 - k]
-        for j in range(1, count):
-            send(remote(slot, slot, first_tx.at[k, j], first_rx.at[k, j], along(1 - k, (heres[1 - k] + j) % count)))
+    s_buf[core, lo] = total
+
+    def units(ring, place, spot, pair):
+        if ring == 0:
+            piece = pl.ds(pl.multiple_of(place % 4 * half_rows, half_rows), half_rows)
+            return s.at[0, place // 4, pl.ds(2 * spot, 2) if pair else spot, piece]
+        if pair:
+            return s.at[1, spot // 2, place, pl.ds(pl.multiple_of(spot % 2 * width, width), width)]
+        return s.at[1, spot // 4, place, pl.ds(pl.multiple_of(spot % 4 * half_rows, half_rows), half_rows)]
+
+    for ring in range(2):
+        slot = units(ring, heres[ring], heres[1 - ring], False)
+        pltpu.make_async_copy(slot, slot, sc_rx.at[ring]).wait()
+        count = counts[1 - ring]
+        for j in sorted(range(1, count), key=lambda j: min(j, count - j)):
+            device = along(1 - ring, (heres[1 - ring] + j) % count)
+            send(remote(slot, slot, first_tx.at[ring, j], first_rx.at[ring, j], device))
 
     for k in range(3):
         send(remote(s_buf.at[core, lo], s_buf.at[core, lo], sg_tx.at[k], sg_rx.at[k], peer(k)))
@@ -178,58 +181,47 @@
                 copy.wait_send()
 
     later.append(cols_sent)
-    cross_near = remote(cross, cross_buf, c_tx.at[0], c_rx.at[0], peer(0))
-    cross_near.start()
     hacc[...] = jnp.zeros_like(hacc)
-    base[...] = jnp.zeros_like(base)
     cross_near.wait()
     cross_buf[...] = cross_buf[...] + cross[...]
     cross_twin = remote(cross_buf, cross_far, c_tx.at[1], c_rx.at[1], peer(1))
     cross_twin.start()
+
+    def pairs(ring):
+        count = counts[1 - ring] // 2
+        return [0] + [k for d in range(1, count) for k in (d, -d) if d < count - d or (d == count - d and k > 0)]
+
+    def sent(ring, way, step, j):
+        half_way, many = counts[ring] // 2, counts[1 - ring] // 2
+        return step < half_way or (step == half_way and j * 2 // many == way)
+
+    def pair_at(ring, j):
+        many = counts[1 - ring] // 2
+        return (heres[1 - ring] // 2 + pairs(ring)[j] + many) % many
+
+    def ring_copy(ring, way, step, j, receiving=False):
+        count, here, sign = counts[ring], heres[ring], 1 - 2 * way
+        place = (here - sign * (step if receiving else step - 1) + count) % count
+        index = (step - 1) * (counts[1 - ring] // 2) + j
+        where = units(ring, place, pair_at(ring, j), True)
+        sems = ring_tx.at[ring, way, index], ring_rx.at[ring, way, index]
+        return remote(where, where, *sems, along(ring, (here + sign + count) % count))
+
+    for j in range(max(nz, ny) // 2):
+        for ring in range(2):
+            count, here = counts[1 - ring], heres[1 - ring]
+            if j >= count // 2:
+                continue
+            for spot in [2 * pair_at(ring, j), 2 * pair_at(ring, j) + 1] if j else [here // 2 * 2 + 1 - here % 2]:
+                where = units(ring, heres[ring], spot, False)
+                k = (here - spot + count) % count
+                remote(where, where, first_tx.at[ring, k], first_rx.at[ring, k], peer(0)).wait_recv()
+            for way in range(2):
+                send(ring_copy(ring, way, 1, j))
+
     for copy in factors:
         copy.wait()
-
-    def sums_here():
-        for k in range(3):
-            mate = mates[k]
-            where = s_buf.at[mate % 2, mate // 2]
-            remote(where, where, sg_tx.at[k], sg_rx.at[k], peer(k)).wait_recv()
-
-    def firsts_here(k):
-        count = counts[1 - k]
-        for j in range(1, count):
-            where = first_slot(k, (heres[1 - k] - j + count) % count)
-            remote(where, where, first_tx.at[k, j], first_rx.at[k, j], peer(0)).wait_recv()
-
-    def cols_here():
-        pltpu.make_async_copy(mine, cols, vc_rx).wait()
-
-
-    def block(ring, place, part):
-        if depth > 1:
-            return s.at[ring, part, place]
-        return s.at[ring, 0, place, pl.ds(part * (run // 2), run // 2)]
-
-    def sent(ring, way, step, part):
-        half_way = counts[ring] // 2
-        return step < half_way or (step == half_way and part == way)
-
-    def ring_copy(ring, way, step, part, receiving=False):
-        count, here, sign = counts[ring], heres[ring], 1 - 2 * way
-        place = (here - sign * (step if receiving else step - 1) + count) % count
-        index = 2 * (step - 1) + (part if step < count // 2 else 0)
-        where = block(ring, place, part)
-        sems = ring_tx.at[ring, way, index], ring_rx.at[ring, way, index]
-        return remote(where, where, *sems, along(ring, (here + sign + count) % count))
-
-    for ring in range(2):
-        firsts_here(ring)
-        for part in range(2):
-            for way in range(2):
-                if sent(ring, way, 1, part):
-                    send(ring_copy(ring, way, 1, part))
-
-    cols_here()
+    pltpu.make_async_copy(mine, cols, vc_rx).wait()
     second = dot(cols[1].astype(F32), f[1], 1, 1, HIGH)
     at[1] = second.astype(BF16)
     cross_twin.wait()
@@ -237,44 +229,58 @@
     first = dot(cols[0].astype(F32) - dot(second, cross[...], 1, 1, HIGH), f[0], 1, 1, HIGH)
     at[0] = first.astype(BF16)
 
-    def apply(ring, place, part):
-        if depth > 1:
-            tail = (part, place)
+    def apply(ring, place):
+        if ring == 0:
+            tail = (place // 4, slice(None), pl.ds(pl.multiple_of(place % 4 * half_rows, half_rows), half_rows))
+            many = ny * half_rows
         else:
-            tail = (0, place, slice(part * (run // 2), (part + 1) * (run // 2)))
-        piece = dot(at[ring], s[(ring, *tail)], 1, 1)
-        if depth > 1:
-            base[part, place] = base[part, place] + piece
-        else:
-            base[0, place, :, tail[2]] = base[0, place, :, tail[2]] + piece
-        piece = piece.astype(BF16)
+            tail = (slice(None), place)
+            many = depth * run
+        piece = dot(at[ring], s[(ring, *tail)].reshape(many, panel), 1, 1).astype(BF16)
         for k in range(2):
-            hacc[k] = hacc[k] + dot(piece, v[(k, *tail)])
-
-    for part in range(2):
+            hacc[k] = hacc[k] + dot(piece, v[(k, *tail)].reshape(many, panel))
+
+    for ring in range(2):
+        apply(ring, heres[ring])
+
+    for step in range(1, max(nz, ny) // 2 + 1):
+        for j in range(max(nz, ny) // 2):
+            for ring in range(2):
+                if j >= counts[1 - ring] // 2:
+                    continue
+                for way in range(2):
+                    if not sent(ring, way, step, j):
+                        continue
+                    ring_copy(ring, way, step, j, receiving=True).wait_recv()
+                    if sent(ring, way, step + 1, j):
+                        send(ring_copy(ring, way, step + 1, j))
         for ring in range(2):
-            apply(ring, heres[ring], part)
-
-    for step in range(1, max(nz, ny) // 2 + 1):
-        for part in range(2):
-            for ring in range(2):
-                for way in range(2):
-                    if not sent(ring, way, step, part):
-                        continue
-                    ring_copy(ring, way, step, part, receiving=True).wait_recv()
-                    if sent(ring, way, step + 1, part):
-                        send(ring_copy(ring, way, step + 1, part))
-                    count, here, sign = counts[ring], heres[ring], 1 - 2 * way
-                    apply(ring, (here - sign * step + count) % count, part)
-
-    sums_here()
+            count, here = counts[ring], heres[ring]
+            for place in (here - step + count, here + step)[: 2 if step < count // 2 else 1]:
+                if step <= count // 2:
+                    apply(ring, place % count)
+
     near = remote(hacc, h_buf, h_tx.at[0], h_rx.at[0], peer(0))
     near.start()
+    pairs_of_places = [(part, place) for part in range(depth) for place in range(0, ny, 2)]
+
+    def right(part, place):
+        spot = slice((part * ny + place) * run, (part * ny + place + 2) * run)
+        update = dot(at[0], s[0, part, place : place + 2].reshape(2 * run, panel), 1, 1)
+        update = update + dot(at[1], s[1, part, place : place + 2].reshape(2 * run, panel), 1, 1)
+        base[:, spot] = a[:, spot].astype(F32) - update
+
     near.wait()
     chip = hacc[...] + h_buf[...]
     h_send[...] = chip.astype(BF16)
     twin = remote(h_send, h_far, h_tx.at[1], h_rx.at[1], peer(1))
     twin.start()
+    for part, place in pairs_of_places:
+        right(part, place)
+    for k in range(3):
+        mate = mates[k]
+        where = s_buf.at[mate % 2, mate // 2]
+        remote(where, where, sg_tx.at[k], sg_rx.at[k], peer(k)).wait_recv()
     rest = s_buf[...].reshape(2, width, panel) - chip
     twin.wait()
     rest = rest - h_far[...].astype(F32)
@@ -282,14 +288,11 @@
     left_two = dot(rest[1] - dot(left_one, cross[...], 1, 0, HIGH), f[1], 1, 0, HIGH)
     left = left_one.astype(BF16), left_two.astype(BF16)
 
-    for part in range(depth):
-        for place in range(0, ny, 2):
-            spot = slice((part * ny + place) * run, (part * ny + place + 2) * run)
-            pair = slice(place, place + 2)
-            update = jnp.concatenate([base[part, place], base[part, place + 1]], axis=1)
-            for k in range(2):
-                update = update + dot(left[k], v[k, part, pair].reshape(2 * run, panel), 1, 1)
-            out[:, spot] = (a[:, spot].astype(F32) - update).astype(BF16)
+    for part, place in pairs_of_places:
+        spot = slice((part * ny + place) * run, (part * ny + place + 2) * run)
+        update = dot(left[0], v[0, part, place : place + 2].reshape(2 * run, panel), 1, 1)
+        update = update + dot(left[1], v[1, part, place : place + 2].reshape(2 * run, panel), 1, 1)
+        out[:, spot] = (base[:, spot] - update).astype(BF16)
 
     for wait in later:
         wait()
@@ -308,7 +311,7 @@
     flops = 2 * rows * width * panel * 10
     result = pl.pallas_call(
         functools.partial(kernel, parts),
-        out_shape=jax.ShapeDtypeStruct((width, rows), BF16),
+        out_shape=pltpu.VMEM((width, rows), BF16),
         in_specs=[hbm] * 5,
         out_specs=pl.BlockSpec(memory_space=pltpu.VMEM),
         scratch_shapes=[
@@ -325,7 +328,7 @@
             pltpu.VMEM((panel, panel), F32),
             pltpu.VMEM((panel, panel), F32),
             pltpu.VMEM((2, width, panel), BF16),
-            pltpu.VMEM((depth, ny, width, 4 * half), F32),
+            pltpu.VMEM((width, rows), F32),
             pltpu.VMEM((2, width, panel), F32),
             pltpu.VMEM((2, width, panel), F32),
             pltpu.VMEM((2, width, panel), BF16),
@@ -346,8 +349,8 @@
             dma((2,)),
             dma((2, most)),
             dma((2, most)),
-            dma((2, 2, most)),
-            dma((2, 2, most)),
+            dma((2, 2, most * most // 4)),
+            dma((2, 2, most * most // 4)),
         ],
         compiler_params=pltpu.CompilerParams(
             collective_id=0, has_side_effects=True, vmem_limit_bytes=56 * 1024 * 1024

time: 67.1 us -> 59.7 us (0.89)
  Pallas kernels: 65 us -> 58.5 us
  local copies, waits for them, and re-layouts: 1.92 us -> 0.82 us
    pallas_call x1, Pallas kernels: 65 us -> 58.5 us  [body(): pl.pallas_call(functools.partial(kernel, parts), out_shape=pltpu.VMEM((wi...]
    unnamed x1, local copies, waits for them, and re-layouts: 1.92 us -> 0.82 us
where the time goes in v3:
time: 59.7 us; the launch traced here: 59.4 us
  Pallas kernels  58.5 us (98%)
  local copies, waits for them, and re-layouts  0.82 us (1%)
    pallas_call x1, Pallas kernels, body(): pl.pallas_call(functools.partial(kernel, parts), out_shape=pltpu.VMEM((wi...  58.5 us

profile of v3, /device:TPU:1, one launch (start us, length us, event | category | flops | bytes accessed | tf_op | source)
XLA Modules:
  0.0 59.4 jit_solution(6609374770662798518)
XLA Ops:
  0.0 58.5 %shard_map.55 = bf16[96,3072]{1,0:T(8,128)(2,1)S(1)} custom-call(bf16[96,3072]{1,0:T(8,128)(2,1)} %bitcast.7, bf16[2,8,192,256]{3,2,1,0:T(8,128)(2,1)} %bitcast.5, bf16[2,8,192,256]{3,2,1,0:T(8,128)(2,1)} %bitcast.6, f32[256,256]{1,0:T(8,128)} %f1_hbm.1, f32[256,256]{1,0:T(8,128)} %f2_hbm.1), custom_call_target="tpu_custom_call" | custom-call | flops 1509949440 | bytes 3145728 | tf_op jit(solution)/shard_map/pallas_call | solution.py:312
  58.6 0.8 %copy.7 = bf16[3072,96]{0,1:T(8,128)(2,1)} copy(bf16[3072,96]{0,1:T(8,128)(2,1)S(1)} %bitcast.4) | data formatting | bytes 1179648

commit v4 on v3

--- a/solution.py
+++ b/solution.py
@@ -25,7 +25,7 @@
     parts,
     a_hbm, v1_hbm, v2_hbm, f1_hbm, f2_hbm,
     out,
-    a, v, f, term, rs_buf, s_buf, unit, s, cols, cross, cross_buf, cross_far, at, base, hacc, h_buf, h_send, h_far,
+    a, v, f, mix, split, h_near, term, term_send, rs_buf, s_buf, unit, s, cols, cross, cross_buf, cross_far, at, base, hacc, h_buf, h_send, h_far,
     load, f_load, rs_tx, rs_rx, vc_tx, vc_rx, sg_tx, sg_rx, sc_tx, sc_rx, c_tx, c_rx, h_tx, h_rx,
     first_tx, first_rx, ring_tx, ring_rx,
 ):
@@ -103,13 +103,14 @@
         sums[k] = more if sums[k] is None else sums[k] + more
     for k in range(2):
         term[k] = sums[k].reshape(2, half_rows, panel)
+        term_send[k] = sums[k].reshape(2, half_rows, panel).astype(BF16)
 
     pl.semaphore_wait(barrier, 3 + (ny - 1) + (nz - 1) + 2 - jnp.where(stays, 1, 0))
 
     scattered = []
     for k in (2, 1, 0):
         mate = mates[k]
-        copy = remote(term.at[mate % 2, mate // 2], rs_buf.at[k], rs_tx.at[k], rs_rx.at[k], peer(k))
+        copy = remote(term_send.at[mate % 2, mate // 2], rs_buf.at[k], rs_tx.at[k], rs_rx.at[k], peer(k))
         send(copy)
         scattered.append(copy)
 
@@ -120,7 +121,7 @@
 
     for copy in scattered:
         copy.wait_recv()
-    total = term[core, lo] + rs_buf[0] + rs_buf[1] + rs_buf[2]
+    total = term[core, lo] + rs_buf[0].astype(F32) + rs_buf[1].astype(F32) + rs_buf[2].astype(F32)
     unit[...] = total.astype(BF16)
 
     landing = s.at[core, slab, y, pl.ds((2 * h + lo) * half_rows, half_rows)]
@@ -219,15 +220,28 @@
             for way in range(2):
                 send(ring_copy(ring, way, 1, j))
 
-    for copy in factors:
-        copy.wait()
-    pltpu.make_async_copy(mine, cols, vc_rx).wait()
-    second = dot(cols[1].astype(F32), f[1], 1, 1, HIGH)
-    at[1] = second.astype(BF16)
-    cross_twin.wait()
-    cross[...] = cross_buf[...] + cross_far[...]
-    first = dot(cols[0].astype(F32) - dot(second, cross[...], 1, 1, HIGH), f[0], 1, 1, HIGH)
-    at[0] = first.astype(BF16)
+    def in_two(values):
+        high = values.astype(BF16)
+        return jnp.concatenate([high, (values - high.astype(F32)).astype(BF16)], axis=0)
+
+    def joined(stacked):
+        return stacked[:width] + stacked[width:]
+
+    def right_factors():
+        for copy in factors:
+            copy.wait()
+        pltpu.make_async_copy(mine, cols, vc_rx).wait()
+        second = dot(cols[1].astype(F32), f[1], 1, 1, HIGH)
+        at[1] = in_two(second)
+        cross_twin.wait()
+        cross[...] = cross_buf[...] + cross_far[...]
+        first = dot(cols[0].astype(F32) - dot(second, cross[...], 1, 1, HIGH), f[0], 1, 1, HIGH)
+        at[0] = in_two(first)
+        mix[...] = dot(dot(f[0], cross[...], 1, 0, HIGH), f[1], 1, 0, HIGH)
+        for k, weights in enumerate((f[0], f[1], mix[...])):
+            high = weights.astype(BF16)
+            split[k, 0] = high
+            split[k, 1] = (weights - high.astype(F32)).astype(BF16)
 
     def apply(ring, place):
         if ring == 0:
@@ -236,12 +250,9 @@
         else:
             tail = (slice(None), place)
             many = depth * run
-        piece = dot(at[ring], s[(ring, *tail)].reshape(many, panel), 1, 1).astype(BF16)
+        piece = in_two(joined(dot(at[ring], s[(ring, *tail)].reshape(many, panel), 1, 1)))
         for k in range(2):
             hacc[k] = hacc[k] + dot(piece, v[(k, *tail)].reshape(many, panel))
-
-    for ring in range(2):
-        apply(ring, heres[ring])
 
     for step in range(1, max(nz, ny) // 2 + 1):
         for j in range(max(nz, ny) // 2):
@@ -254,13 +265,19 @@
                     ring_copy(ring, way, step, j, receiving=True).wait_recv()
                     if sent(ring, way, step + 1, j):
                         send(ring_copy(ring, way, step + 1, j))
+        if step == 1:
+            right_factors()
+            for ring in range(2):
+                apply(ring, heres[ring])
         for ring in range(2):
             count, here = counts[ring], heres[ring]
             for place in (here - step + count, here + step)[: 2 if step < count // 2 else 1]:
                 if step <= count // 2:
                     apply(ring, place % count)
 
-    near = remote(hacc, h_buf, h_tx.at[0], h_rx.at[0], peer(0))
+    own = hacc[:, :width] + hacc[:, width:]
+    h_near[...] = own.astype(BF16)
+    near = remote(h_near, h_buf, h_tx.at[0], h_rx.at[0], peer(0))
     near.start()
     pairs_of_places = [(part, place) for part in range(depth) for place in range(0, ny, 2)]
 
@@ -268,24 +285,34 @@
         spot = slice((part * ny + place) * run, (part * ny + place + 2) * run)
         update = dot(at[0], s[0, part, place : place + 2].reshape(2 * run, panel), 1, 1)
         update = update + dot(at[1], s[1, part, place : place + 2].reshape(2 * run, panel), 1, 1)
-        base[:, spot] = a[:, spot].astype(F32) - update
-
+        base[:, spot] = a[:, spot].astype(F32) - joined(update)
+
+    many = len(pairs_of_places) // 2
+    for part, place in pairs_of_places[:many]:
+        right(part, place)
     near.wait()
-    chip = hacc[...] + h_buf[...]
+    chip = own + h_buf[...].astype(F32)
     h_send[...] = chip.astype(BF16)
     twin = remote(h_send, h_far, h_tx.at[1], h_rx.at[1], peer(1))
     twin.start()
-    for part, place in pairs_of_places:
-        right(part, place)
     for k in range(3):
         mate = mates[k]
         where = s_buf.at[mate % 2, mate // 2]
         remote(where, where, sg_tx.at[k], sg_rx.at[k], peer(k)).wait_recv()
-    rest = s_buf[...].reshape(2, width, panel) - chip
+    for part, place in pairs_of_places[many:]:
+        right(part, place)
+    for wait in later:
+        wait()
+    here_rest = s_buf[...].reshape(2, width, panel) - chip
+    left_one = dot(here_rest[0], f[0], 1, 0, HIGH)
+    left_two = dot(here_rest[1], f[1], 1, 0, HIGH) - dot(here_rest[0], mix[...], 1, 0, HIGH)
     twin.wait()
-    rest = rest - h_far[...].astype(F32)
-    left_one = dot(rest[0], f[0], 1, 0, HIGH)
-    left_two = dot(rest[1] - dot(left_one, cross[...], 1, 0, HIGH), f[1], 1, 0, HIGH)
+
+    def times(k, panel_id):
+        return dot(h_far[panel_id], split[k, 0]) + dot(h_far[panel_id], split[k, 1])
+
+    left_one = left_one - times(0, 0)
+    left_two = left_two - (times(1, 1) - times(2, 0))
     left = left_one.astype(BF16), left_two.astype(BF16)
 
     for part, place in pairs_of_places:
@@ -293,9 +320,6 @@
         update = dot(left[0], v[0, part, place : place + 2].reshape(2 * run, panel), 1, 1)
         update = update + dot(left[1], v[1, part, place : place + 2].reshape(2 * run, panel), 1, 1)
         out[:, spot] = (base[:, spot] - update).astype(BF16)
-
-    for wait in later:
-        wait()
 
 
 def body(parts, matrix, vectors_one, factor_one, vectors_two, factor_two):
@@ -318,8 +342,12 @@
             pltpu.VMEM((width, rows), BF16),
             pltpu.VMEM((2, *grid, panel), BF16),
             pltpu.VMEM((2, panel, panel), F32),
+            pltpu.VMEM((panel, panel), F32),
+            pltpu.VMEM((3, 2, panel, panel), BF16),
+            pltpu.VMEM((2, width, panel), BF16),
             pltpu.VMEM((2, 2, half, panel), F32),
-            pltpu.VMEM((3, half, panel), F32),
+            pltpu.VMEM((2, 2, half, panel), BF16),
+            pltpu.VMEM((3, half, panel), BF16),
             pltpu.VMEM((2, 2, half, panel), F32),
             pltpu.VMEM((half, panel), BF16),
             pltpu.VMEM((2, *grid, panel), BF16),
@@ -327,10 +355,10 @@
             pltpu.VMEM((panel, panel), F32),
             pltpu.VMEM((panel, panel), F32),
             pltpu.VMEM((panel, panel), F32),
-            pltpu.VMEM((2, width, panel), BF16),
+            pltpu.VMEM((2, 2 * width, panel), BF16),
             pltpu.VMEM((width, rows), F32),
-            pltpu.VMEM((2, width, panel), F32),
-            pltpu.VMEM((2, width, panel), F32),
+            pltpu.VMEM((2, 2 * width, panel), F32),
+            pltpu.VMEM((2, width, panel), BF16),
             pltpu.VMEM((2, width, panel), BF16),
             pltpu.VMEM((2, width, panel), BF16),
             dma((1 + 2 * depth,)),

time: 59.7 us -> 57.7 us (0.966)
  Pallas kernels: 58.5 us -> 56.7 us
    pallas_call x1, Pallas kernels: 58.5 us -> 56.7 us  [body(): pl.pallas_call(functools.partial(kernel, parts), out_shape=pltpu.VMEM((wi...]
where the time goes in v4:
time: 57.7 us; the launch traced here: 57.6 us
  Pallas kernels  56.7 us (98%)
  local copies, waits for them, and re-layouts  0.82 us (1%)
    pallas_call x1, Pallas kernels, body(): pl.pallas_call(functools.partial(kernel, parts), out_shape=pltpu.VMEM((wi...  56.7 us

profile of v4, /device:TPU:1, one launch (start us, length us, event | category | flops | bytes accessed | tf_op | source)
XLA Modules:
  0.0 57.6 jit_solution(16734310978597004598)
XLA Ops:
  0.0 56.7 %shard_map.55 = bf16[96,3072]{1,0:T(8,128)(2,1)S(1)} custom-call(bf16[96,3072]{1,0:T(8,128)(2,1)} %bitcast.7, bf16[2,8,192,256]{3,2,1,0:T(8,128)(2,1)} %bitcast.5, bf16[2,8,192,256]{3,2,1,0:T(8,128)(2,1)} %bitcast.6, f32[256,256]{1,0:T(8,128)} %f1_hbm.1, f32[256,256]{1,0:T(8,128)} %f2_hbm.1), custom_call_target="tpu_custom_call" | custom-call | flops 1509949440 | bytes 3145728 | tf_op jit(solution)/shard_map/pallas_call | solution.py:336
  56.7 0.8 %copy.7 = bf16[3072,96]{0,1:T(8,128)(2,1)} copy(bf16[3072,96]{0,1:T(8,128)(2,1)S(1)} %bitcast.4) | data formatting | bytes 1179648

commit v5 on v4

--- a/solution.py
+++ b/solution.py
@@ -36,8 +36,9 @@
     run = 4 * half_rows
     p = lax.axis_index("prow")
     q = lax.axis_index("pcol")
-    z, y, h = q // (ny * nh), (q // nh) % ny, q % nh
-    lo, core = p // 2, p % 2
+    rem, quo = lax.rem, lax.div
+    z, y, h = quo(q, ny * nh), rem(quo(q, nh), ny), rem(q, nh)
+    lo, core = quo(p, 2), rem(p, 2)
     mates = (2 * lo + 1 - core, 2 * (1 - lo) + core, 3 - p)
 
     def at_device(row, zi, yi, hi):
@@ -57,22 +58,76 @@
         copy.start()
         later.append(copy.wait_send)
 
-    owner, slab = z // depth, z % depth
+    owner, slab = quo(z, depth), rem(z, depth)
     counts, heres = (nz, ny), (z, y)
 
     def along(ring, place):
         return at_device(p, place, y, h) if ring == 0 else at_device(p, z, place, h)
 
+    def z_of(number, row):
+        part, piece = quo(number, 4), rem(number, 4)
+        reach = 2 * rem(rem(piece, 2) + quo(row, 2), 2) + quo(piece, 2)
+        return rem(row * depth + part + (2 * part - 1) * reach + 2 * nz, nz)
+
+    def unit_of(place):
+        d = rem(place - p * depth + nz, nz)
+        part = 1 - quo(rem(d + nz - 1, nz), 4) if depth > 1 else 0
+        reach = part * (d - 1) + (1 - part) * rem(nz - d, nz)
+        return part * 4 + 2 * rem(reach, 2) + rem(quo(reach, 2) + lo, 2)
+
     number = slab * 4 + 2 * h + lo
-    stays = (owner == p) & (number == z)
-    from_z, from_h, from_lo = p * depth + z // 4, z % 4 // 2, z % 2
-
-    halves = [(k, part) for part in range(depth) for k in range(2)]
-    loads = [pltpu.make_async_copy(a_hbm, a, load.at[0])]
-    for place, (k, part) in enumerate(halves):
-        loads.append(pltpu.make_async_copy((v1_hbm, v2_hbm)[k].at[part], v.at[k, part], load.at[1 + place]))
-    for copy in loads:
-        copy.start()
+    to_z = z_of(number, owner)
+    stays = (owner == p) & (to_z == z)
+    own = unit_of(z)
+    from_z, from_h, from_lo = p * depth + quo(own, 4), quo(rem(own, 4), 2), rem(own, 2)
+    spots = y, own
+
+    known = {}
+
+    def once(key, make):
+        if key not in known:
+            known[key] = make()
+        return known[key]
+
+    def place_at(ring, offset):
+        count = counts[ring]
+        return once((ring, offset % count), lambda: rem(heres[ring] + offset % count, count))
+
+    def home(offset):
+        def make():
+            unit_number = unit_of(place_at(0, offset))
+            return quo(unit_number, 4), pl.multiple_of(rem(unit_number, 4) * half_rows, half_rows)
+
+        return once(("home", offset % nz), make)
+
+    def pair_at(ring, j):
+        many = counts[1 - ring] // 2
+        shift = ([0, 1] if many < 4 else [0, 1, 3, 2])[j]
+        return once(("pair", ring, j), lambda: rem(quo(spots[ring], 2) + shift, many))
+
+    def pair_rows(j):
+        make = lambda: (quo(pair_at(1, j), 2), pl.multiple_of(rem(pair_at(1, j), 2) * width, width))
+        return once(("rows", j), make)
+
+    def place_of(ring, spot):
+        return spot if ring == 0 else z_of(spot, p)
+
+    stretch = ny * run
+    cuts = [(part, cut) for part in range(depth) for cut in range(2)]
+    a_loads = []
+    v_loads = []
+    for place, (part, cut) in enumerate(cuts):
+        lanes = slice((2 * part + cut) * stretch // 2, (2 * part + cut + 1) * stretch // 2)
+        middle = slice(cut * ny // 2, (cut + 1) * ny // 2)
+        a_loads.append(pltpu.make_async_copy(a_hbm.at[:, lanes], a.at[:, lanes], load.at[0, place]))
+        v_loads.append(
+            [
+                pltpu.make_async_copy(source.at[part, middle], v.at[k, part, middle], load.at[1 + k, place])
+                for k, source in enumerate((v1_hbm, v2_hbm))
+            ]
+        )
+        for copy in (a_loads[-1], *v_loads[-1]):
+            copy.start()
     factors = [pltpu.make_async_copy((f1_hbm, f2_hbm)[k], f.at[k], f_load.at[k]) for k in range(2)]
     for copy in factors:
         copy.start()
@@ -86,7 +141,7 @@
         greet(peer(k))
     for ring in range(2):
         for k in range(1, counts[ring]):
-            greet(along(ring, (heres[ring] + k) % counts[ring]))
+            greet(along(ring, place_at(ring, k)))
     for k in range(2):
         from_p = 2 * from_lo + k
 
@@ -94,13 +149,15 @@
         def _():
             greet(at_device(from_p, from_z, y, from_h))
 
-    stretch = ny * run
     sums = [None, None]
-    loads[0].wait()
-    for place, (k, part) in enumerate(halves):
-        loads[1 + place].wait()
-        more = dot(a[:, part * stretch : (part + 1) * stretch], v[k, part].reshape(stretch, panel))
-        sums[k] = more if sums[k] is None else sums[k] + more
+    for place, (part, cut) in enumerate(cuts):
+        lanes = slice((2 * part + cut) * stretch // 2, (2 * part + cut + 1) * stretch // 2)
+        a_loads[place].wait()
+        for k in range(2):
+            v_loads[place][k].wait()
+            vectors = v[k, part, cut * ny // 2 : (cut + 1) * ny // 2].reshape(stretch // 2, panel)
+            more = dot(a[:, lanes], vectors)
+            sums[k] = more if sums[k] is None else sums[k] + more
     for k in range(2):
         term[k] = sums[k].reshape(2, half_rows, panel)
         term_send[k] = sums[k].reshape(2, half_rows, panel).astype(BF16)
@@ -114,53 +171,59 @@
         send(copy)
         scattered.append(copy)
 
+    for copy in scattered:
+        copy.wait_recv()
+    total = term[core, lo] + rs_buf[0].astype(F32) + rs_buf[1].astype(F32) + rs_buf[2].astype(F32)
+    unit[...] = total.astype(BF16)
+
+    landing = s.at[core, slab, y, pl.ds((2 * h + lo) * half_rows, half_rows)]
+    far_unit = remote(unit, landing, sc_tx.at[0], sc_rx.at[core], at_device(owner, to_z, y, 1 - h))
+    near_unit = remote(unit, landing, sc_tx.at[1], sc_rx.at[core], at_device(owner, to_z, y, h))
+    near_local = pltpu.make_async_copy(unit, landing, sc_rx.at[core])
+    send(far_unit)
+
+    @pl.when(stays)
+    def _():
+        near_local.start()
+
+    @pl.when(jnp.logical_not(stays))
+    def _():
+        near_unit.start()
+
+    def near_sent():
+        @pl.when(jnp.logical_not(stays))
+        def _():
+            near_unit.wait_send()
+
+    later.append(near_sent)
+
+    s_buf[core, lo] = total
+
     rows = depth * stretch
     cross[...] = dot(v[0].reshape(rows, panel), v[1].reshape(rows, panel), 0, 0)
     cross_near = remote(cross, cross_buf, c_tx.at[0], c_rx.at[0], peer(0))
     cross_near.start()
 
-    for copy in scattered:
-        copy.wait_recv()
-    total = term[core, lo] + rs_buf[0].astype(F32) + rs_buf[1].astype(F32) + rs_buf[2].astype(F32)
-    unit[...] = total.astype(BF16)
-
-    landing = s.at[core, slab, y, pl.ds((2 * h + lo) * half_rows, half_rows)]
-    far_unit = remote(unit, landing, sc_tx.at[0], sc_rx.at[core], at_device(owner, number, y, 1 - h))
-    near_unit = remote(unit, landing, sc_tx.at[1], sc_rx.at[core], at_device(owner, number, y, h))
-    near_local = pltpu.make_async_copy(unit, landing, sc_rx.at[core])
-    send(far_unit)
-
-    @pl.when(stays)
-    def _():
-        near_local.start()
-
-    @pl.when(jnp.logical_not(stays))
-    def _():
-        near_unit.start()
-
-    def near_sent():
-        @pl.when(jnp.logical_not(stays))
-        def _():
-            near_unit.wait_send()
-
-    later.append(near_sent)
-
-    s_buf[core, lo] = total
-
-    def units(ring, place, spot, pair):
+    def units(ring, offset, spot):
         if ring == 0:
-            piece = pl.ds(pl.multiple_of(place % 4 * half_rows, half_rows), half_rows)
-            return s.at[0, place // 4, pl.ds(2 * spot, 2) if pair else spot, piece]
-        if pair:
-            return s.at[1, spot // 2, place, pl.ds(pl.multiple_of(spot % 2 * width, width), width)]
-        return s.at[1, spot // 4, place, pl.ds(pl.multiple_of(spot % 4 * half_rows, half_rows), half_rows)]
+            part, first = home(offset)
+            return s.at[0, part, spot, pl.ds(first, half_rows)]
+        first = pl.multiple_of(rem(spot, 4) * half_rows, half_rows)
+        return s.at[1, quo(spot, 4), place_at(1, offset), pl.ds(first, half_rows)]
+
+    def two_units(ring, offset, j):
+        if ring == 0:
+            part, first = home(offset)
+            return s.at[0, part, pl.ds(2 * pair_at(0, j), 2), pl.ds(first, half_rows)]
+        part, first = pair_rows(j)
+        return s.at[1, part, place_at(1, offset), pl.ds(first, width)]
 
     for ring in range(2):
-        slot = units(ring, heres[ring], heres[1 - ring], False)
+        slot = units(ring, 0, spots[ring])
         pltpu.make_async_copy(slot, slot, sc_rx.at[ring]).wait()
         count = counts[1 - ring]
         for j in sorted(range(1, count), key=lambda j: min(j, count - j)):
-            device = along(1 - ring, (heres[1 - ring] + j) % count)
+            device = along(1 - ring, place_at(1 - ring, j))
             send(remote(slot, slot, first_tx.at[ring, j], first_rx.at[ring, j], device))
 
     for k in range(3):
@@ -188,34 +251,26 @@
     cross_twin = remote(cross_buf, cross_far, c_tx.at[1], c_rx.at[1], peer(1))
     cross_twin.start()
 
-    def pairs(ring):
-        count = counts[1 - ring] // 2
-        return [0] + [k for d in range(1, count) for k in (d, -d) if d < count - d or (d == count - d and k > 0)]
-
     def sent(ring, way, step, j):
         half_way, many = counts[ring] // 2, counts[1 - ring] // 2
         return step < half_way or (step == half_way and j * 2 // many == way)
 
-    def pair_at(ring, j):
-        many = counts[1 - ring] // 2
-        return (heres[1 - ring] // 2 + pairs(ring)[j] + many) % many
-
     def ring_copy(ring, way, step, j, receiving=False):
-        count, here, sign = counts[ring], heres[ring], 1 - 2 * way
-        place = (here - sign * (step if receiving else step - 1) + count) % count
+        sign = 1 - 2 * way
         index = (step - 1) * (counts[1 - ring] // 2) + j
-        where = units(ring, place, pair_at(ring, j), True)
+        where = two_units(ring, -sign * (step if receiving else step - 1), j)
         sems = ring_tx.at[ring, way, index], ring_rx.at[ring, way, index]
-        return remote(where, where, *sems, along(ring, (here + sign + count) % count))
+        return remote(where, where, *sems, along(ring, place_at(ring, sign)))
 
     for j in range(max(nz, ny) // 2):
         for ring in range(2):
             count, here = counts[1 - ring], heres[1 - ring]
             if j >= count // 2:
                 continue
-            for spot in [2 * pair_at(ring, j), 2 * pair_at(ring, j) + 1] if j else [here // 2 * 2 + 1 - here % 2]:
-                where = units(ring, heres[ring], spot, False)
-                k = (here - spot + count) % count
+            mine_too = once(("odd", ring), lambda: rem(spots[ring], 2))
+            for spot in [2 * pair_at(ring, j) + 1 - mine_too] + ([2 * pair_at(ring, j) + mine_too] if j else []):
+                where = units(ring, 0, spot)
+                k = rem(here - place_of(ring, spot) + count, count)
                 remote(where, where, first_tx.at[ring, k], first_rx.at[ring, k], peer(0)).wait_recv()
             for way in range(2):
                 send(ring_copy(ring, way, 1, j))
@@ -243,19 +298,22 @@
             split[k, 0] = high
             split[k, 1] = (weights - high.astype(F32)).astype(BF16)
 
-    def apply(ring, place):
+    def apply(ring, offset):
         if ring == 0:
-            tail = (place // 4, slice(None), pl.ds(pl.multiple_of(place % 4 * half_rows, half_rows), half_rows))
+            part, first = home(offset)
+            tail = (part, slice(None), pl.ds(first, half_rows))
             many = ny * half_rows
         else:
-            tail = (slice(None), place)
+            tail = (slice(None), place_at(1, offset))
             many = depth * run
         piece = in_two(joined(dot(at[ring], s[(ring, *tail)].reshape(many, panel), 1, 1)))
         for k in range(2):
             hacc[k] = hacc[k] + dot(piece, v[(k, *tail)].reshape(many, panel))
 
-    for step in range(1, max(nz, ny) // 2 + 1):
-        for j in range(max(nz, ny) // 2):
+    ready = [right_factors, *(functools.partial(apply, ring, 0) for ring in range(2))]
+    turns = max(nz, ny) // 2
+    for step in range(1, turns + 1):
+        for j in range(turns):
             for ring in range(2):
                 if j >= counts[1 - ring] // 2:
                     continue
@@ -265,18 +323,19 @@
                     ring_copy(ring, way, step, j, receiving=True).wait_recv()
                     if sent(ring, way, step + 1, j):
                         send(ring_copy(ring, way, step + 1, j))
-        if step == 1:
-            right_factors()
-            for ring in range(2):
-                apply(ring, heres[ring])
+            if step == 1 and j == 0:
+                continue
+            for _ in range(-(-len(ready) // (turns - j))):
+                ready.pop(0)()
         for ring in range(2):
-            count, here = counts[ring], heres[ring]
-            for place in (here - step + count, here + step)[: 2 if step < count // 2 else 1]:
-                if step <= count // 2:
-                    apply(ring, place % count)
-
-    own = hacc[:, :width] + hacc[:, width:]
-    h_near[...] = own.astype(BF16)
+            half_way = counts[ring] // 2
+            for offset in (-step, step)[: 2 if step < half_way else 1 if step == half_way else 0]:
+                ready.append(functools.partial(apply, ring, offset))
+    for work in ready:
+        work()
+
+    summed = hacc[:, :width] + hacc[:, width:]
+    h_near[...] = summed.astype(BF16)
     near = remote(h_near, h_buf, h_tx.at[0], h_rx.at[0], peer(0))
     near.start()
     pairs_of_places = [(part, place) for part in range(depth) for place in range(0, ny, 2)]
@@ -291,7 +350,7 @@
     for part, place in pairs_of_places[:many]:
         right(part, place)
     near.wait()
-    chip = own + h_buf[...].astype(F32)
+    chip = summed + h_buf[...].astype(F32)
     h_send[...] = chip.astype(BF16)
     twin = remote(h_send, h_far, h_tx.at[1], h_rx.at[1], peer(1))
     twin.start()
@@ -313,13 +372,13 @@
 
     left_one = left_one - times(0, 0)
     left_two = left_two - (times(1, 1) - times(2, 0))
-    left = left_one.astype(BF16), left_two.astype(BF16)
+    left = in_two(left_one), in_two(left_two)
 
     for part, place in pairs_of_places:
         spot = slice((part * ny + place) * run, (part * ny + place + 2) * run)
         update = dot(left[0], v[0, part, place : place + 2].reshape(2 * run, panel), 1, 1)
         update = update + dot(left[1], v[1, part, place : place + 2].reshape(2 * run, panel), 1, 1)
-        out[:, spot] = (base[:, spot] - update).astype(BF16)
+        out[:, spot] = (base[:, spot] - joined(update)).astype(BF16)
 
 
 def body(parts, matrix, vectors_one, factor_one, vectors_two, factor_two):
@@ -361,7 +420,7 @@
             pltpu.VMEM((2, width, panel), BF16),
             pltpu.VMEM((2, width, panel), BF16),
             pltpu.VMEM((2, width, panel), BF16),
-            dma((1 + 2 * depth,)),
+            dma((3, 2 * depth)),
             dma((2,)),
             dma((3,)),
             dma((3,)),

time: 57.7 us -> 58 us (level)
  no operation moved by 1% of the time
where the time goes in v5:
time: 58 us; the launch traced here: 57.9 us
  Pallas kernels  57 us (98%)
  local copies, waits for them, and re-layouts  0.82 us (1%)
    pallas_call x1, Pallas kernels, body(): pl.pallas_call(functools.partial(kernel, parts), out_shape=pltpu.VMEM((wi...  57 us

profile of v5, /device:TPU:1, one launch (start us, length us, event | category | flops | bytes accessed | tf_op | source)
XLA Modules:
  0.0 57.9 jit_solution(7848430507331072915)
XLA Ops:
  0.0 57.0 %shard_map.55 = bf16[96,3072]{1,0:T(8,128)(2,1)S(1)} custom-call(bf16[96,3072]{1,0:T(8,128)(2,1)} %bitcast.7, bf16[2,8,192,256]{3,2,1,0:T(8,128)(2,1)} %bitcast.5, bf16[2,8,192,256]{3,2,1,0:T(8,128)(2,1)} %bitcast.6, f32[256,256]{1,0:T(8,128)} %f1_hbm.1, f32[256,256]{1,0:T(8,128)} %f2_hbm.1), custom_call_target="tpu_custom_call" | custom-call | flops 1509949440 | bytes 3145728 | tf_op jit(solution)/shard_map/pallas_call | solution.py:395
  57.0 0.8 %copy.7 = bf16[3072,96]{0,1:T(8,128)(2,1)} copy(bf16[3072,96]{0,1:T(8,128)(2,1)S(1)} %bitcast.4) | data formatting | bytes 1179648

commit v6 on v5

--- a/solution.py
+++ b/solution.py
@@ -372,13 +372,13 @@
 
     left_one = left_one - times(0, 0)
     left_two = left_two - (times(1, 1) - times(2, 0))
-    left = in_two(left_one), in_two(left_two)
+    left = left_one.astype(BF16), left_two.astype(BF16)
 
     for part, place in pairs_of_places:
         spot = slice((part * ny + place) * run, (part * ny + place + 2) * run)
         update = dot(left[0], v[0, part, place : place + 2].reshape(2 * run, panel), 1, 1)
         update = update + dot(left[1], v[1, part, place : place + 2].reshape(2 * run, panel), 1, 1)
-        out[:, spot] = (base[:, spot] - joined(update)).astype(BF16)
+        out[:, spot] = (base[:, spot] - update).astype(BF16)
 
 
 def body(parts, matrix, vectors_one, factor_one, vectors_two, factor_two):

time: 58 us -> 57.6 us (level)
  no operation moved by 1% of the time
where the time goes in v6:
time: 57.6 us; the launch traced here: 57.5 us
  Pallas kernels  56.7 us (98%)
  local copies, waits for them, and re-layouts  0.82 us (1%)
    pallas_call x1, Pallas kernels, body(): pl.pallas_call(functools.partial(kernel, parts), out_shape=pltpu.VMEM((wi...  56.7 us

profile of v6, /device:TPU:1, one launch (start us, length us, event | category | flops | bytes accessed | tf_op | source)
XLA Modules:
  0.0 57.5 jit_solution(10633683441885730747)
XLA Ops:
  0.0 56.7 %shard_map.55 = bf16[96,3072]{1,0:T(8,128)(2,1)S(1)} custom-call(bf16[96,3072]{1,0:T(8,128)(2,1)} %bitcast.7, bf16[2,8,192,256]{3,2,1,0:T(8,128)(2,1)} %bitcast.5, bf16[2,8,192,256]{3,2,1,0:T(8,128)(2,1)} %bitcast.6, f32[256,256]{1,0:T(8,128)} %f1_hbm.1, f32[256,256]{1,0:T(8,128)} %f2_hbm.1), custom_call_target="tpu_custom_call" | custom-call | flops 1509949440 | bytes 3145728 | tf_op jit(solution)/shard_map/pallas_call | solution.py:395
  56.7 0.8 %copy.7 = bf16[3072,96]{0,1:T(8,128)(2,1)} copy(bf16[3072,96]{0,1:T(8,128)(2,1)S(1)} %bitcast.4) | data formatting | bytes 1179648
